TPU v7x, 512 devices: a whole 4x8x8 slice. The times are simulated.
512 devices in a mesh: dp: 64 (over y, x, core), tensor: 8 (over z).
Axes of the slice: x: 4, y: 8, z: 8, core: 2. Of those that a mesh axis runs over, the one named last changes fastest.
Arguments:
- features: bfloat16 [16384, 3072], P('dp', 'tensor'), may hold values from -6 to 6
- out_grad: bfloat16 [16384, 1024], P('dp', 'tensor'), may hold values from -1.1953125 to 1.1953125
- weight: bfloat16 [3072, 1024], P('dp', 'tensor'), may hold values from -0.109375 to 0.109375
- feedback: float32 [196608, 1024], P('dp', 'tensor'), may hold values from -12 to 12
- warm_basis: float32 [1024, 32], P('tensor'), may hold values from -6 to 6
Outputs:
- input_grad: bfloat16 [16384, 3072], P('dp', 'tensor')
- new_feedback: float32 [196608, 1024], P('dp', 'tensor')
- new_basis: float32 [1024, 32], P('tensor')
All inputs are finite; a program needn't handle non-finite values.
Results may differ from a plain program's by a relative error of at most 0.017.
Values may be sent and summed in bfloat16 or wider, within the bound.
No kernel may reach another device: no remote copies, remote signals or barrier semaphores. Data moves between devices by JAX's collectives and lax.ppermute only.
A program may use at most 64 MiB of HBM per device.

v0:
```python
import jax
import jax.numpy as jnp
from jax import lax
from jax.sharding import PartitionSpec as P


def on_device(features, out_grad, weight, feedback, warm_basis):
    highest = lax.Precision.HIGHEST
    replicas = lax.axis_size("dp")
    grads = lax.dot_general(
        lax.all_gather(features, "tensor", axis=1, tiled=True),
        out_grad,
        (((0,), (0,)), ((), ())),
        preferred_element_type=jnp.float32,
    )
    merged = grads + feedback
    partial_value = lax.dot_general(
        out_grad,
        lax.all_gather(weight, "dp", axis=0, tiled=True),
        (((1,), (1,)), ((), ())),
        preferred_element_type=jnp.float32,
    )
    input_grad = lax.psum_scatter(
        partial_value.astype(jnp.bfloat16), "tensor", scatter_dimension=1, tiled=True
    )
    local_left = jnp.dot(merged, warm_basis, precision=highest)
    left = lax.psum(local_left, "dp") / replicas
    gram_matrix = jnp.dot(left.T, left, precision=highest)
    factor = jnp.linalg.cholesky(gram_matrix)
    basis = jax.scipy.linalg.solve_triangular(factor, left.T, lower=True).T
    local_right = lax.dot_general(merged, basis, (((0,), (0,)), ((), ())), precision=highest)
    right = lax.psum(local_right, "dp") / replicas
    approx = jnp.dot(basis, right.T, precision=highest)
    new_feedback = merged - approx
    return (input_grad, new_feedback, right)


def solution(mesh):
    return jax.shard_map(
        on_device,
        mesh=mesh,
        in_specs=(
            P("dp", "tensor"),
            P("dp", "tensor"),
            P("dp", "tensor"),
            P("dp", "tensor"),
            P("tensor", None),
        ),
        out_specs=(P("dp", "tensor"), P("dp", "tensor"), P("tensor", None)),
        check_vma=False,
    )
```

profile of v0, /device:TPU:1, one launch (start us, length us, event | category | flops | bytes accessed | tf_op | source)
XLA Modules:
  0.0 530.8 jit_solution(5595900233849746358)
XLA Ops:
  7.2 0.0 copy-start
  7.2 0.0 all-gather.2.cloned.1.call-start
  7.2 0.7 all-gather.2.cloned.1.call-update
  7.9 0.0 all-reduce.2.cloned.1.call-start
  8.0 59.8 %all_gather.6 = bf16[3072,128]{1,0:T(8,128)(2,1)} all-gather(bf16[48,128]{1,0:T(8,128)(2,1)} %param.7), channel_id=1, replica_groups=mesh['dp'=64,'tensor'=8] {'dp'}, dimensions={0}, use_global_device_ids=true | all-gather | bytes 798720 | tf_op jit(solution)/shard_map/all_gather | solution.py:19
  67.8 0.0 copy-start.2
  67.8 0.0 all-gather.2.cloned.1.call-done
  67.8 0.0 copy-done
  67.8 2.5 convolution_add_fusion
  70.3 0.0 copy-done.2
  70.3 2.4 fusion.11
  72.7 0.0 all-reduce.2.cloned.1.call-update
  72.7 0.0 reduce-scatter.4.cloned.1.call-start
  72.8 1.7 convolution_convert_fusion
  74.5 1.6 copy.10
  76.1 0.0 reduce-scatter.4.cloned.1.call-update
  76.1 185.8 %all-reduce.2.cloned.1.call-done = f32[3072,32]{0,1:T(8,128)} async-done(((f32[3072,32]{0,1:T(8,128)}), f32[3072,32]{0,1:T(8,128)}) %all-reduce.2.cloned.1.call-update) | async-done | bytes 393232 | tf_op jit(solution)/shard_map/psum | solution.py:27
  261.9 1.6 fusion.2
  263.5 0.1 copy.9
  263.6 2.9 cholesky.16
  266.5 0.6 compare_reduce_fusion
  267.2 0.7 fusion.6
  267.8 2.4 custom-call.7
  270.3 1.5 fusion
  271.8 1.0 fusion.12
  272.8 246.0 %psum.15 = f32[128,32]{0,1:T(8,128)S(1)} all-reduce(f32[128,32]{0,1:T(8,128)S(1)} %fusion.12), channel_id=1, replica_groups=mesh['dp'=64,'tensor'=8] {'dp'}, use_global_device_ids=true, to_apply=%region_4.5 | all-reduce | flops 4096 | bytes 32768 | tf_op jit(solution)/shard_map/psum | solution.py:32
  518.8 0.0 copy-start.1
  518.8 3.8 convolution_subtract_fusion
  522.6 0.0 copy-done.1
  522.6 0.0 reduce-scatter.4.cloned.1.call-done
  522.6 1.7 copy.11
  (3 shorter events, 0.0 us)
Async XLA Ops:
  7.2 60.6 %copy-start = (bf16[256,128]{1,0:T(8,128)(2,1)S(1)}, bf16[256,128]{1,0:T(8,128)(2,1)}, u32[]{:S(2)}) copy-start(bf16[256,128]{1,0:T(8,128)(2,1)} %param.6) | copy-start | bytes 196612
  7.2 60.6 %all-gather.2.cloned.1.call-start = ((), (), s32[]{:S(2)}) async-start(), calls=%async_computation.1 | async-start | bytes 1769472 | tf_op jit(solution)/shard_map/all_gather | solution.py:11
  7.9 254.0 %all-reduce.2.cloned.1.call-start = ((), (), s32[]{:S(2)}) async-start(), calls=%async_computation.2 | async-start | bytes 786432 | tf_op jit(solution)/shard_map/psum | solution.py:27
  67.8 2.5 copy-start.2
  72.7 449.8 %reduce-scatter.4.cloned.1.call-start = ((), (), s32[]{:S(2)}) async-start(), calls=%async_computation.3 | async-start | bytes 1769472
  518.8 3.8 copy-start.1
Sparse Core Ops, SparseCore 0:
  10.1 44.7 all-gather.1
  72.9 189.0 all-reduce.1
  265.0 40.6 reduce-scatter.3
where the time goes:
time: 535 us; the launch traced here: 531 us
  blocking collectives  306 us (57%)
  waiting for transfers between devices  187 us (35%)
  matrix products  14.5 us (3%)
  between operations  13.8 us (3%)
  other arithmetic  6.69 us (1%)
    psum x1, blocking collectives, on_device(): right = lax.psum(local_right, 'dp') / replicas  246 us
    psum x1, waiting for transfers between devices, on_device(): left = lax.psum(local_left, 'dp') / replicas  186 us
    all_gather x1, blocking collectives, on_device(): lax.all_gather(weight, 'dp', axis=0, tiled=True)  59.8 us
  transfers between devices with their start and end apart: 3, of which 1 were waited for; matrix products, arithmetic and copies ran while one was open for 3% of the time, Pallas kernels for 0%

commit v1 on v0

v1 whole, which is shorter than its diff:
```python
import jax
import jax.numpy as jnp
from jax import lax
from jax.experimental import pallas as pl
from jax.experimental.pallas import tpu as pltpu
from jax.sharding import Mesh, PartitionSpec as P

BF = jnp.bfloat16
F32 = jnp.float32
HIGHEST = lax.Precision.HIGHEST
CHIPS = ("y", "x")
DP = ("y", "x", "core")
N_Z = 8
N_CHIP = 32
REPLICAS = 64
D_IN = 3072
HALF = D_IN // 2
SLAB = D_IN // N_Z
PIECE = D_IN // REPLICAS
TOK = 256
COLS = 128
RANK = 32


def dot(a, b, dims, precision=None):
    return lax.dot_general(a, b, (dims, ((), ())), precision=precision, preferred_element_type=F32)


def partial_kernel(out_grad_ref, weight_ref, out_ref):
    for chip in range(4):
        for core in range(2):
            rows = weight_ref[core, chip]
            at = (chip * 2 + core) * PIECE
            out_ref[0, at : at + PIECE, :] = dot(rows, out_grad_ref[...], ((1,), (1,))).astype(BF)


def partial_call(out_grad, weight):
    return pl.pallas_call(
        partial_kernel,
        grid=(N_Z,),
        in_specs=[
            pl.BlockSpec((TOK, COLS), lambda z: (0, 0)),
            pl.BlockSpec((2, 4, PIECE, COLS), lambda z: (0, z, 0, 0)),
        ],
        out_specs=pl.BlockSpec((1, SLAB, TOK), lambda z: (z, 0, 0)),
        out_shape=jax.ShapeDtypeStruct((N_Z, SLAB, TOK), BF),
        cost_estimate=pl.CostEstimate(flops=2 * TOK * COLS * D_IN, bytes_accessed=2500000, transcendentals=0),
        name="partial_rows",
    )(out_grad, weight)


def merged_kernel(core_ref, features_ref, out_grad_ref, feedback_ref, merged_ref, send_ref, keep_ref):
    step = pl.program_id(0)
    merged = dot(features_ref[0], out_grad_ref[...], ((0,), (0,))) + feedback_ref[...]
    merged_ref[...] = merged

    @pl.when(step < N_Z // 2)
    def _():
        send_ref[...] = merged.astype(BF)

    @pl.when(step >= N_Z // 2)
    def _():
        keep_ref[...] = merged


def merged_call(core, features, out_grad, feedback):
    half = N_Z // 2

    def slab(step, core_ref):
        first = (1 - core_ref[0]) * half
        return lax.rem(first + step, N_Z)

    return pl.pallas_call(
        merged_kernel,
        grid_spec=pltpu.PrefetchScalarGridSpec(
            num_scalar_prefetch=1,
            grid=(N_Z,),
            in_specs=[
                pl.BlockSpec((1, TOK, SLAB), lambda s, c: (slab(s, c), 0, 0)),
                pl.BlockSpec((TOK, COLS), lambda s, c: (0, 0)),
                pl.BlockSpec((SLAB, COLS), lambda s, c: (slab(s, c), 0)),
            ],
            out_specs=[
                pl.BlockSpec((SLAB, COLS), lambda s, c: (slab(s, c), 0)),
                pl.BlockSpec((SLAB, COLS), lambda s, c: (jnp.minimum(s, half - 1), 0)),
                pl.BlockSpec((SLAB, COLS), lambda s, c: (jnp.maximum(s - half, 0), 0)),
            ],
        ),
        out_shape=[
            jax.ShapeDtypeStruct((D_IN, COLS), F32),
            jax.ShapeDtypeStruct((HALF, COLS), BF),
            jax.ShapeDtypeStruct((HALF, COLS), F32),
        ],
        cost_estimate=pl.CostEstimate(flops=2 * TOK * COLS * D_IN, bytes_accessed=6000000, transcendentals=0),
        name="merged_rows",
    )(core, features, out_grad, feedback)


def mean_kernel(parts_ref, out_ref):
    total = parts_ref[0].astype(F32)
    for chip in range(1, N_CHIP):
        total += parts_ref[chip].astype(F32)
    rounded = (total * (1.0 / REPLICAS)).astype(BF)
    for chip in range(N_CHIP):
        out_ref[chip] = rounded


def mean_call(parts):
    return pl.pallas_call(
        mean_kernel,
        out_shape=jax.ShapeDtypeStruct((N_CHIP, PIECE, COLS), BF),
        cost_estimate=pl.CostEstimate(flops=N_CHIP * PIECE * COLS, bytes_accessed=800000, transcendentals=0),
        name="mean_rows",
    )(parts)


def tail_kernel(mean_ref, merged_ref, warm_ref, fresh_ref, right_ref):
    mean = mean_ref[...]
    warm = warm_ref[...]
    outer = dot(mean, mean, ((0,), (0,)))
    right = dot(warm, outer, ((1,), (0,)), HIGHEST)
    gram = dot(right, warm, ((1,), (1,)), HIGHEST)
    row_at = lax.broadcasted_iota(jnp.int32, (RANK, 1), 0)
    for k in range(RANK):
        scale = lax.rsqrt(gram[k : k + 1, k : k + 1])
        column = jnp.where(row_at > k, gram[:, k : k + 1] * scale, 0.0)
        own = row_at == k
        gram_row = gram[k : k + 1] * scale
        right_row = right[k : k + 1] * scale
        warm_row = warm[k : k + 1] * scale
        gram = jnp.where(own, gram_row, gram - column * gram_row)
        right = jnp.where(own, right_row, right - column * right_row)
        warm = jnp.where(own, warm_row, warm - column * warm_row)
    right_ref[...] = right
    mix = dot(warm, right, ((0,), (0,)), HIGHEST)
    high = mix.astype(BF)
    low = (mix - high.astype(F32)).astype(BF)
    for slab in range(N_Z):
        rows = pl.ds(slab * SLAB, SLAB)
        block = mean_ref[rows, :]
        approx = dot(block, high, ((1,), (0,))) + dot(block, low, ((1,), (0,)))
        fresh_ref[rows, :] = merged_ref[rows, :] - approx


def tail_call(mean, merged, warm):
    return pl.pallas_call(
        tail_kernel,
        out_shape=[
            jax.ShapeDtypeStruct((D_IN, COLS), F32),
            jax.ShapeDtypeStruct((RANK, COLS), F32),
        ],
        cost_estimate=pl.CostEstimate(flops=6 * COLS * COLS * D_IN, bytes_accessed=4000000, transcendentals=32),
        name="basis_and_feedback",
    )(mean, merged, warm)


def to_all_chips(block):
    spread = lax.optimization_barrier(jnp.broadcast_to(block[None], (N_CHIP,) + block.shape))
    return lax.all_to_all(spread, CHIPS, 0, 0)


def on_device(features, out_grad, weight, feedback, warm_basis):
    core = lax.axis_index("core").astype(jnp.int32).reshape(1)
    gathered = lax.all_gather(features, "z", axis=0)
    weights = lax.all_gather(to_all_chips(weight), "core", axis=0)
    partial_rows = partial_call(out_grad, weights)
    input_grad = lax.psum_scatter(partial_rows, "z", scatter_dimension=0, tiled=False).T

    merged, send, keep = merged_call(core, gathered, out_grad, feedback)
    other = lax.ppermute(send, "core", [(0, 1), (1, 0)])
    chip_sum = (keep + other.astype(F32)).astype(BF).reshape(N_CHIP, PIECE, COLS)
    parts = lax.all_to_all(chip_sum, CHIPS, 0, 0)
    spread = mean_call(parts)
    half_mean = lax.all_to_all(spread, CHIPS, 0, 0).reshape(HALF, COLS)
    mean = lax.all_gather(half_mean, "core", axis=0, tiled=True)
    new_feedback, right = tail_call(mean, merged, warm_basis.T)
    return (input_grad, new_feedback, right.T)


def solution(mesh):
    grid = Mesh(mesh.devices.reshape(8, 4, 2, 8), ("y", "x", "core", "z"))
    return jax.shard_map(
        on_device,
        mesh=grid,
        in_specs=(P(DP, "z"), P(DP, "z"), P(DP, "z"), P(DP, "z"), P("z", None)),
        out_specs=(P(DP, "z"), P(DP, "z"), P("z", None)),
        check_vma=False,
    )
```

time: 535 us -> 134 us (0.25)
  blocking collectives: 306 us -> 57.3 us
  waiting for transfers between devices: 187 us -> 24.5 us
  Pallas kernels: 0 us -> 22.1 us
  matrix products: 14.5 us -> 0 us
  starting transfers between devices: 0.12 us -> 11.8 us
  other arithmetic: 6.69 us -> 1.21 us
    psum x1 -> x0, blocking collectives: 246 us -> none  [on_device(): right = lax.psum(local_right, 'dp') / replicas]
    psum x1 -> x0, waiting for transfers between devices: 186 us -> none  [on_device(): left = lax.psum(local_left, 'dp') / replicas]
    all_gather x1 -> x2, blocking collectives: 59.8 us -> 10.1 us  [the longest x1 5.51 us: on_device(): mean = lax.all_gather(half_mean, 'core', axis=0, tiled=True)]
    all_to_all x0 -> x2, blocking collectives: none -> 47.1 us  [the longest x1 24.1 us: to_all_chips(): return lax.all_to_all(spread, CHIPS, 0, 0)]
    pallas_call x0 -> x4, Pallas kernels: none -> 22.1 us  [the longest x1 7.04 us: merged_call(): pl.pallas_call(merged_kernel, grid_spec=pltpu.PrefetchScalarGridSpec(num_...]
    dot_general x6 -> x0, matrix products: 13 us -> none  [the longest x1 3.77 us: on_device(): approx = jnp.dot(basis, right.T, precision=highest)]
    all_gather x1, waiting for transfers between devices: 0.02 us -> 11.2 us  [on_device(): gathered = lax.all_gather(features, 'z', axis=0)]
    all_to_all x0 -> x1, waiting for transfers between devices: none -> 11.1 us  [on_device(): half_mean = lax.all_to_all(spread, CHIPS, 0, 0).reshape(HALF, COLS)]
  transfers between devices with their start and end apart: 3 -> 4, of which waited for: 1 -> 3; matrix products, arithmetic and copies ran while one was open for 3% -> 3% of each run, Pallas kernels for 0% -> 11%
where the time goes in v1:
time: 134 us; the launch traced here: 133 us
  blocking collectives  57.3 us (43%)
  waiting for transfers between devices  24.5 us (18%)
  Pallas kernels  22.1 us (16%)
  between operations  14.1 us (11%)
  starting transfers between devices  11.8 us (9%)
  local copies, waits for them, and re-layouts  2.5 us (2%)
    all_to_all x1, blocking collectives, to_all_chips(): return lax.all_to_all(spread, CHIPS, 0, 0)  24.1 us
    all_to_all x1, blocking collectives, on_device(): parts = lax.all_to_all(chip_sum, CHIPS, 0, 0)  23 us
    all_gather x1, waiting for transfers between devices, on_device(): gathered = lax.all_gather(features, 'z', axis=0)  11.2 us
    all_to_all x1, waiting for transfers between devices, on_device(): half_mean = lax.all_to_all(spread, CHIPS, 0, 0).reshape(HALF, COLS)  11.1 us
    pallas_call x1, Pallas kernels, merged_call(): pl.pallas_call(merged_kernel, grid_spec=pltpu.PrefetchScalarGridSpec(num_...  7.04 us
    pallas_call x1, Pallas kernels, tail_call(): pl.pallas_call(tail_kernel, out_shape=[jax.ShapeDtypeStruct((D_IN, COLS),...  7.01 us
    ppermute x1, starting transfers between devices, on_device(): other = lax.ppermute(send, 'core', [(0, 1), (1, 0)])  6.71 us
    pallas_call x1, Pallas kernels, partial_call(): pl.pallas_call(partial_kernel, grid=(N_Z,), in_specs=[pl.BlockSpec((TOK,...  6.26 us
  transfers between devices with their start and end apart: 4, of which 3 were waited for; matrix products, arithmetic and copies ran while one was open for 3% of the time, Pallas kernels for 11%

profile of v1, /device:TPU:1, one launch (start us, length us, event | category | flops | bytes accessed | tf_op | source)
XLA Modules:
  0.0 133.5 jit_solution(838426291024242191)
XLA Ops:
  7.2 0.0 all-gather.4.cloned.1.call-start
  7.2 0.7 all-gather.4.cloned.1.call-update
  7.9 0.0 reduce-scatter.2.cloned.1.call-start
  7.9 0.8 broadcast_in_dim.2
  8.7 24.1 %all_to_all.15 = bf16[32,48,128]{2,1,0:T(8,128)(2,1)S(1)} all-to-all(bf16[32,48,128]{2,1,0:T(8,128)(2,1)S(1)} %broadcast_in_dim.2), channel_id=1, replica_groups=mesh['y'=8,'x'=4,'core'=2,'z'=8] {'y','x'}, dimensions={0} | all-to-all | bytes 786432 | tf_op jit(solution)/shard_map/all_to_all | solution.py:159
  32.8 4.6 %all-gather = bf16[64,48,128]{2,1,0:T(8,128)(2,1)} all-gather(bf16[32,48,128]{2,1,0:T(8,128)(2,1)S(1)} %all_to_all.15), channel_id=2, replica_groups=mesh['y'=8,'x'=4,'core'=2,'z'=8] {'core'}, dimensions={0}, use_global_device_ids=true | all-gather | bytes 1179648 | tf_op jit(solution)/shard_map/all_gather | solution.py:165
  37.4 6.3 %partial_rows.1 = bf16[8,384,256]{2,1,0:T(8,128)(2,1)} custom-call(bf16[256,128]{1,0:T(8,128)(2,1)} %out_grad_ref.3, bf16[2,32,48,128]{3,2,1,0:T(8,128)(2,1)} %bitcast.10), custom_call_target="tpu_custom_call" | custom-call | flops 201326592 | bytes 2500000 | tf_op jit(solution)/shard_map/partial_rows/pallas_call | solution.py:38
  43.7 0.0 reduce-scatter.2.cloned.1.call-update
  43.7 11.2 %all-gather.4.cloned.1.call-done = bf16[2048,384]{1,0:T(8,128)(2,1)} async-done(((bf16[256,384]{1,0:T(8,128)(2,1)}), bf16[2048,384]{1,0:T(8,128)(2,1)}) %all-gather.4.cloned.1.call-update) | async-done | bytes 1572880 | tf_op jit(solution)/shard_map/all_gather | solution.py:164
  54.9 7.0 %merged_rows.1 = (f32[3072,128]{1,0:T(8,128)}, bf16[1536,128]{1,0:T(8,128)(2,1)}, f32[1536,128]{1,0:T(8,128)}) custom-call(s32[1]{0:T(128)} %bitcast.3.core_ref, bf16[8,256,384]{2,1,0:T(8,128)(2,1)} %bitcast.13, bf16[256,128]{1,0:T(8,128)(2,1)} %out_grad_ref.3, f32[3072,128]{1,0:T(8,128)} %feedback_ref.1), custom_call_target="tpu_custom_call" | custom-call | flops 201326592 | bytes 6000000 | tf_op jit(solution)/shard_map/merged_rows/pallas_call | solution.py:73
  61.9 6.7 %collective-permute-start = (bf16[1536,128]{1,0:T(8,128)(2,1)}, bf16[1536,128]{1,0:T(8,128)(2,1)S(1)}, u32[]{:S(2)}, u32[]{:S(2)}) collective-permute-start(bf16[1536,128]{1,0:T(8,128)(2,1)} %get-tuple-element.9), channel_id=1, source_target_pairs={{0,8},{8,0},{1,9},{9,1},{2,10},{10,2},{3,11},{11,3},{4,12},{12,4},... | collective-permute-start | bytes 1179656 | tf_op jit(solution)/shard_map/ppermute | solution.py:170
  68.7 1.5 %collective-permute-done = bf16[1536,128]{1,0:T(8,128)(2,1)S(1)} collective-permute-done((bf16[1536,128]{1,0:T(8,128)(2,1)}, bf16[1536,128]{1,0:T(8,128)(2,1)S(1)}, u32[]{:S(2)}, u32[]{:S(2)}) %collective-permute-start) | collective-permute-done | bytes 393248 | tf_op jit(solution)/shard_map/ppermute | solution.py:170
  70.2 1.2 add_convert_fusion
  71.4 23.0 %all_to_all.16.parts_ref = bf16[32,48,128]{2,1,0:T(8,128)(2,1)} all-to-all(bf16[32,48,128]{2,1,0:T(8,128)(2,1)S(1)} %bitcast.12), channel_id=1, replica_groups=mesh['y'=8,'x'=4,'core'=2,'z'=8] {'y','x'}, dimensions={0} | all-to-all | bytes 786432 | tf_op jit(solution)/shard_map/all_to_all | solution.py:172
  94.4 1.8 %mean_rows.1 = bf16[32,48,128]{2,1,0:T(8,128)(2,1)} custom-call(bf16[32,48,128]{2,1,0:T(8,128)(2,1)} %all_to_all.16.parts_ref), custom_call_target="tpu_custom_call" | custom-call | flops 196608 | bytes 800000 | tf_op jit(solution)/shard_map/mean_rows/pallas_call | solution.py:109
  96.3 5.0 %all-to-all-start.2 = ((bf16[32,48,128]{2,1,0:T(8,128)(2,1)}), bf16[32,48,128]{2,1,0:T(8,128)(2,1)S(1)}, u32[]{:S(2)}, u32[]{:S(2)}) async-start(bf16[32,48,128]{2,1,0:T(8,128)(2,1)} %mean_rows.1), calls=%async_computation.3 | async-start | bytes 786432 | tf_op jit(solution)/shard_map/all_to_all | solution.py:174
  101.3 0.0 reduce-scatter.2.cloned.1.call-done
  101.3 1.7 %copy.9 = bf16[256,384]{1,0:T(8,128)(2,1)} copy(bf16[256,384]{0,1:T(8,128)(2,1)} %bitcast.14) | data formatting | bytes 393216
  103.0 11.1 %all-to-all-done.2 = bf16[32,48,128]{2,1,0:T(8,128)(2,1)S(1)} async-done(((bf16[32,48,128]{2,1,0:T(8,128)(2,1)}), bf16[32,48,128]{2,1,0:T(8,128)(2,1)S(1)}, u32[]{:S(2)}, u32[]{:S(2)}) %all-to-all-start.2) | async-done | bytes 393248 | tf_op jit(solution)/shard_map/all_to_all | solution.py:174
  114.1 5.5 %all_gather.19.mean_ref = bf16[3072,128]{1,0:T(8,128)(2,1)} all-gather(bf16[1536,128]{1,0:T(8,128)(2,1)S(1)} %bitcast.11), channel_id=1, replica_groups=mesh['y'=8,'x'=4,'core'=2,'z'=8] {'core'}, dimensions={0}, use_global_device_ids=true | all-gather | bytes 1179648 | tf_op jit(solution)/shard_map/all_gather | solution.py:175
  119.6 7.0 %basis_and_feedback.1 = (f32[3072,128]{1,0:T(8,128)}, f32[32,128]{1,0:T(8,128)}) custom-call(bf16[3072,128]{1,0:T(8,128)(2,1)} %all_gather.19.mean_ref, f32[3072,128]{1,0:T(8,128)} %get-tuple-element.10.merged_ref, f32[32,128]{1,0:T(8,128)} %bitcast.15), custom_call_target="tpu_custom_call" | custom-call | flops 301989888 | bytes 4000000 | tf_op jit(solution)/shard_map/basis_and_feedback/pallas_call | solution.py:146
Async XLA Ops:
  7.2 47.7 %all-gather.4.cloned.1.call-start = ((), (), s32[]{:S(2)}) async-start(), calls=%async_computation.5 | async-start | bytes 1769472 | tf_op jit(solution)/shard_map/all_gather | solution.py:164
  7.9 93.4 %reduce-scatter.2.cloned.1.call-start = ((), (), s32[]{:S(2)}) async-start(), calls=%async_computation.4 | async-start | bytes 1769472 | tf_op jit(solution)/shard_map/reduce_scatter | solution.py:167
  61.9 8.3 %collective-permute-start = (bf16[1536,128]{1,0:T(8,128)(2,1)}, bf16[1536,128]{1,0:T(8,128)(2,1)S(1)}, u32[]{:S(2)}, u32[]{:S(2)}) collective-permute-start(bf16[1536,128]{1,0:T(8,128)(2,1)} %get-tuple-element.9), channel_id=1, source_target_pairs={{0,8},{8,0},{1,9},{9,1},{2,10},{10,2},{3,11},{11,3},{4,12},{12,4},... | collective-permute-start | bytes 1179656 | tf_op jit(solution)/shard_map/ppermute | solution.py:170
  96.3 17.8 %all-to-all-start.2 = ((bf16[32,48,128]{2,1,0:T(8,128)(2,1)}), bf16[32,48,128]{2,1,0:T(8,128)(2,1)S(1)}, u32[]{:S(2)}, u32[]{:S(2)}) async-start(bf16[32,48,128]{2,1,0:T(8,128)(2,1)} %mean_rows.1), calls=%async_computation.3 | async-start | bytes 786432 | tf_op jit(solution)/shard_map/all_to_all | solution.py:174
Sparse Core Ops, SparseCore 0:
  10.1 44.7 all-gather.3
  58.3 42.2 reduce-scatter.1

commit v2 on v1

v2 whole, which is shorter than its diff:
```python
import jax
import jax.numpy as jnp
from jax import lax
from jax.experimental import pallas as pl
from jax.experimental.pallas import tpu as pltpu
from jax.sharding import Mesh, PartitionSpec as P

BF = jnp.bfloat16
F32 = jnp.float32
HIGHEST = lax.Precision.HIGHEST
CHIPS = ("y", "x")
DP = ("y", "x", "core")
N_Z = 8
N_CHIP = 32
REPLICAS = 64
D_IN = 3072
HALF = D_IN // 2
SLAB = D_IN // N_Z
PIECE = D_IN // REPLICAS
TOK = 256
COLS = 128
RANK = 32


def dot(a, b, dims, precision=None):
    return lax.dot_general(a, b, (dims, ((), ())), precision=precision, preferred_element_type=F32)


def partial_kernel(out_grad_ref, weight_ref, out_ref):
    rows = [weight_ref[core, chip] for chip in range(4) for core in range(2)]
    slab = jnp.concatenate(rows, axis=0)
    out_ref[0] = dot(out_grad_ref[...], slab, ((1,), (1,))).astype(BF)


def partial_call(out_grad, weight):
    return pl.pallas_call(
        partial_kernel,
        grid=(N_Z,),
        in_specs=[
            pl.BlockSpec((TOK, COLS), lambda z: (0, 0)),
            pl.BlockSpec((2, 4, PIECE, COLS), lambda z: (0, z, 0, 0)),
        ],
        out_specs=pl.BlockSpec((1, TOK, SLAB), lambda z: (z, 0, 0)),
        out_shape=jax.ShapeDtypeStruct((N_Z, TOK, SLAB), BF),
        cost_estimate=pl.CostEstimate(flops=2 * TOK * COLS * D_IN, bytes_accessed=2500000, transcendentals=0),
        name="partial_slabs",
    )(out_grad, weight)


def tail_kernel(mean_ref, merged_ref, warm_ref, fresh_ref, right_ref, merged_buf, fresh_buf, in_sems, out_sems):
    bands = merged_buf.shape[0]
    band = D_IN // bands
    loads = [
        pltpu.make_async_copy(merged_ref.at[pl.ds(i * band, band)], merged_buf.at[i], in_sems.at[i])
        for i in range(bands)
    ]
    stores = [
        pltpu.make_async_copy(fresh_buf.at[i], fresh_ref.at[pl.ds(i * band, band)], out_sems.at[i])
        for i in range(bands)
    ]
    for load in loads:
        load.start()
    mean = mean_ref[...]
    warm = warm_ref[...]
    outer = dot(mean, mean, ((0,), (0,)))
    right = dot(warm, outer, ((1,), (0,)), HIGHEST)
    gram = dot(right, warm, ((1,), (1,)), HIGHEST)
    row_at = lax.broadcasted_iota(jnp.int32, (RANK, 1), 0)
    for k in range(RANK):
        scale = lax.rsqrt(gram[k : k + 1, k : k + 1])
        column = jnp.where(row_at > k, gram[:, k : k + 1] * scale, 0.0)
        own = row_at == k
        gram_row = gram[k : k + 1] * scale
        right_row = right[k : k + 1] * scale
        warm_row = warm[k : k + 1] * scale
        gram = jnp.where(own, gram_row, gram - column * gram_row)
        right = jnp.where(own, right_row, right - column * right_row)
        warm = jnp.where(own, warm_row, warm - column * warm_row)
    right_ref[...] = right
    mix = dot(warm, right, ((0,), (0,)), HIGHEST)
    high = mix.astype(BF)
    low = (mix - high.astype(F32)).astype(BF)
    for i in range(bands):
        block = mean_ref[i * band : (i + 1) * band, :]
        approx = dot(block, high, ((1,), (0,))) + dot(block, low, ((1,), (0,)))
        loads[i].wait()
        fresh_buf[i] = merged_buf[i] - approx
        stores[i].start()
    for store in stores:
        store.wait()


def tail_call(mean, merged, warm):
    bands = 4
    in_vmem = pl.BlockSpec(memory_space=pltpu.VMEM)
    in_hbm = pl.BlockSpec(memory_space=pl.ANY)
    return pl.pallas_call(
        tail_kernel,
        in_specs=[in_vmem, in_hbm, in_vmem],
        out_specs=[in_hbm, in_vmem],
        out_shape=[
            jax.ShapeDtypeStruct((D_IN, COLS), F32),
            jax.ShapeDtypeStruct((RANK, COLS), F32),
        ],
        scratch_shapes=[
            pltpu.VMEM((bands, D_IN // bands, COLS), F32),
            pltpu.VMEM((bands, D_IN // bands, COLS), F32),
            pltpu.SemaphoreType.DMA((bands,)),
            pltpu.SemaphoreType.DMA((bands,)),
        ],
        cost_estimate=pl.CostEstimate(flops=6 * COLS * COLS * D_IN, bytes_accessed=4000000, transcendentals=32),
        name="basis_and_feedback",
    )(mean, merged, warm)


def to_all_chips(block):
    spread = lax.optimization_barrier(jnp.broadcast_to(block[None], (N_CHIP,) + block.shape))
    return lax.all_to_all(spread, CHIPS, 0, 0)


def swap_cores(block):
    return lax.ppermute(block, "core", [(0, 1), (1, 0)])


def on_device(features, out_grad, weight, feedback, warm_basis):
    core = lax.axis_index("core")
    gathered = lax.all_gather(features, ("core", "z"), axis=0).reshape(2, N_Z, TOK, SLAB)

    weights = lax.all_gather(to_all_chips(weight), "core", axis=0)
    partial_slabs = partial_call(out_grad, weights)
    pair_out_grad = lax.all_gather(out_grad, "core", axis=0)
    other_half = swap_cores(lax.dynamic_slice_in_dim(feedback, (1 - core) * HALF, HALF))
    own_half = lax.dynamic_slice_in_dim(feedback, core * HALF, HALF)
    chip_feedback = lax.optimization_barrier(own_half + other_half)
    input_grad = lax.psum_scatter(partial_slabs, "z", scatter_dimension=0, tiled=False)

    half_features = lax.dynamic_slice_in_dim(gathered, core * (N_Z // 2), N_Z // 2, axis=1)
    chip_grad = jnp.einsum("szta,stb->zab", half_features, pair_out_grad, preferred_element_type=F32)
    chip_sum = (chip_grad.reshape(HALF, COLS) + chip_feedback).astype(BF)
    parts = lax.all_to_all(chip_sum.reshape(N_CHIP, PIECE, COLS), CHIPS, 0, 0)

    own_features = lax.dynamic_index_in_dim(gathered, core, 0, keepdims=False)
    grad = jnp.einsum("zta,tb->zab", own_features, out_grad, preferred_element_type=F32)
    merged = grad.reshape(D_IN, COLS) + feedback

    piece = (jnp.sum(parts.astype(F32), axis=0) / REPLICAS).astype(BF)
    half_mean = to_all_chips(piece).reshape(HALF, COLS)
    mean = lax.all_gather(half_mean, "core", axis=0, tiled=True)
    new_feedback, right = tail_call(mean, merged, warm_basis.T)
    return (input_grad, new_feedback, right.T)


def solution(mesh):
    grid = Mesh(mesh.devices.reshape(8, 4, 2, 8), ("y", "x", "core", "z"))
    return jax.shard_map(
        on_device,
        mesh=grid,
        in_specs=(P(DP, "z"), P(DP, "z"), P(DP, "z"), P(DP, "z"), P("z", None)),
        out_specs=(P(DP, "z"), P(DP, "z"), P("z", None)),
        check_vma=False,
    )
```

time: 134 us -> 127 us (0.948)
  blocking collectives: 57.3 us -> 35.3 us
  Pallas kernels: 22.1 us -> 13.9 us
  starting transfers between devices: 11.8 us -> 18.2 us
  waiting for transfers between devices: 24.5 us -> 30.8 us
  matrix products: 0 us -> 5.14 us
  local copies, waits for them, and re-layouts: 2.5 us -> 6.75 us
  between operations: 14.1 us -> 15.6 us
    all_to_all x2 -> x1, blocking collectives: 47.1 us -> 23.2 us  [on_device(): parts = lax.all_to_all(chip_sum.reshape(N_CHIP, PIECE, COLS), CHIPS, 0, 0)]
    all_to_all x1 -> x2, starting transfers between devices: 4.97 us -> 15.3 us  [to_all_chips(): return lax.all_to_all(spread, CHIPS, 0, 0)]
    pallas_call x3 -> x1, Pallas kernels: 15.9 us -> 7.67 us  [tail_call(): pl.pallas_call(tail_kernel, in_specs=[in_vmem, in_hbm, in_vmem], out_spec...]
    dot_general x0 -> x2, matrix products: none -> 5.14 us  [the longest x1 3.13 us: on_device(): jnp.einsum('zta,tb->zab', own_features, out_grad, preferred_element_type=...]
    all_gather x1, waiting for transfers between devices: 11.2 us -> 15.8 us  [on_device(): lax.all_gather(features, ('core', 'z'), axis=0).reshape(2, N_Z, TOK, SLAB)]
    ppermute x1, starting transfers between devices: 6.71 us -> 2.88 us  [swap_cores(): return lax.ppermute(block, 'core', [(0, 1), (1, 0)])]
    dot_general x0 -> x2, local copies, waits for them, and re-layouts: none -> 3.22 us  [on_device(): jnp.einsum('zta,tb->zab', own_features, out_grad, preferred_element_type=...]
    all_to_all x1 -> x2, waiting for transfers between devices: 11.1 us -> 14.2 us  [to_all_chips(): return lax.all_to_all(spread, CHIPS, 0, 0)]
  transfers between devices with their start and end apart: 4 -> 5, of which waited for: 3 -> 3; matrix products, arithmetic and copies ran while one was open for 3% -> 10% of each run, Pallas kernels for 11% -> 11%
where the time goes in v2:
time: 127 us; the launch traced here: 126 us
  blocking collectives  35.3 us (28%)
  waiting for transfers between devices  30.8 us (24%)
  starting transfers between devices  18.2 us (14%)
  between operations  15.6 us (12%)
  Pallas kernels  13.9 us (11%)
  local copies, waits for them, and re-layouts  6.75 us (5%)
  matrix products  5.14 us (4%)
    all_to_all x1, blocking collectives, on_device(): parts = lax.all_to_all(chip_sum.reshape(N_CHIP, PIECE, COLS), CHIPS, 0, 0)  23.2 us
    all_gather x1, waiting for transfers between devices, on_device(): lax.all_gather(features, ('core', 'z'), axis=0).reshape(2, N_Z, TOK, SLAB)  15.8 us
    all_to_all x2, starting transfers between devices, to_all_chips(): return lax.all_to_all(spread, CHIPS, 0, 0)  15.3 us
    all_to_all x2, waiting for transfers between devices, to_all_chips(): return lax.all_to_all(spread, CHIPS, 0, 0)  14.2 us
    pallas_call x1, Pallas kernels, tail_call(): pl.pallas_call(tail_kernel, in_specs=[in_vmem, in_hbm, in_vmem], out_spec...  7.67 us
    pallas_call x1, Pallas kernels, partial_call(): pl.pallas_call(partial_kernel, grid=(N_Z,), in_specs=[pl.BlockSpec((TOK,...  6.2 us
    all_gather x1, blocking collectives, on_device(): mean = lax.all_gather(half_mean, 'core', axis=0, tiled=True)  5.53 us
    all_gather x1, blocking collectives, on_device(): weights = lax.all_gather(to_all_chips(weight), 'core', axis=0)  4.6 us
  transfers between devices with their start and end apart: 5, of which 3 were waited for; matrix products, arithmetic and copies ran while one was open for 10% of the time, Pallas kernels for 11%

profile of v2, /device:TPU:1, one launch (start us, length us, event | category | flops | bytes accessed | tf_op | source)
XLA Modules:
  0.0 125.9 jit_solution(12154532960921224201)
XLA Ops:
  8.0 0.0 copy-start.1
  8.0 0.0 all-gather.5.cloned.1.call-start
  8.1 0.7 all-gather.5.cloned.1.call-update
  8.7 1.5 %broadcast_in_dim.4 = bf16[32,48,128]{2,1,0:T(8,128)(2,1)} broadcast(bf16[48,128]{1,0:T(8,128)(2,1)} %param.7), dimensions={1,2} | broadcast | bytes 405504 | tf_op jit(solution)/shard_map/broadcast_in_dim | solution.py:117
  10.2 10.5 %all-to-all-start = ((bf16[32,48,128]{2,1,0:T(8,128)(2,1)}), bf16[32,48,128]{2,1,0:T(8,128)(2,1)S(1)}, u32[]{:S(2)}, u32[]{:S(2)}) async-start(bf16[32,48,128]{2,1,0:T(8,128)(2,1)} %broadcast_in_dim.4), calls=%async_computation | async-start | bytes 786432 | tf_op jit(solution)/shard_map/all_to_all | solution.py:118
  20.8 0.0 reduce-scatter.2.cloned.1.call-start
  20.8 1.2 constant_dynamic-slice_fusion
  22.0 2.9 %collective-permute-start = (f32[1536,128]{1,0:T(8,128)S(1)}, f32[1536,128]{1,0:T(8,128)S(1)}, u32[]{:S(2)}, u32[]{:S(2)}) collective-permute-start(f32[1536,128]{1,0:T(8,128)S(1)} %constant_dynamic-slice_fusion), channel_id=1, source_target_pairs={{0,8},{8,0},{1,9},{9,1},{2,10},{10,2},{3,11},{11,3},{4,12},{12,4},... | collective-permute-start | bytes 2359304 | tf_op jit(solution)/shard_map/ppermute | solution.py:122
  24.9 0.0 copy-done.1
  24.9 2.0 %all-gather.2 = bf16[512,128]{1,0:T(8,128)(2,1)S(1)} all-gather(bf16[256,128]{1,0:T(8,128)(2,1)S(1)} %copy-done.1), channel_id=4, replica_groups=mesh['y'=8,'x'=4,'core'=2,'z'=8] {'core'}, dimensions={0}, use_global_device_ids=true | all-gather | bytes 196608 | tf_op jit(solution)/shard_map/all_gather | solution.py:131
  26.9 7.7 %all-to-all-done = bf16[32,48,128]{2,1,0:T(8,128)(2,1)S(1)} async-done(((bf16[32,48,128]{2,1,0:T(8,128)(2,1)}), bf16[32,48,128]{2,1,0:T(8,128)(2,1)S(1)}, u32[]{:S(2)}, u32[]{:S(2)}) %all-to-all-start) | async-done | bytes 393248 | tf_op jit(solution)/shard_map/all_to_all | solution.py:118
  34.6 4.6 %all-gather = bf16[64,48,128]{2,1,0:T(8,128)(2,1)} all-gather(bf16[32,48,128]{2,1,0:T(8,128)(2,1)S(1)} %all-to-all-done), channel_id=2, replica_groups=mesh['y'=8,'x'=4,'core'=2,'z'=8] {'core'}, dimensions={0}, use_global_device_ids=true | all-gather | bytes 1179648 | tf_op jit(solution)/shard_map/all_gather | solution.py:129
  39.2 0.0 copy-start
  39.2 6.2 %partial_slabs.1 = bf16[8,256,384]{2,1,0:T(8,128)(2,1)} custom-call(bf16[256,128]{1,0:T(8,128)(2,1)} %out_grad_ref.1, bf16[2,32,48,128]{3,2,1,0:T(8,128)(2,1)} %bitcast.30), custom_call_target="tpu_custom_call" | custom-call | flops 201326592 | bytes 2500000 | tf_op jit(solution)/shard_map/partial_slabs/pallas_call | solution.py:36
  45.4 0.0 reduce-scatter.2.cloned.1.call-update
  45.4 0.0 collective-permute-done
  45.4 0.0 copy-done
  45.4 0.1 dynamic-slice_add_fusion
  45.5 15.8 %all-gather.5.cloned.1.call-done = bf16[4096,384]{1,0:T(8,128)(2,1)} async-done(((bf16[256,384]{1,0:T(8,128)(2,1)}), bf16[4096,384]{1,0:T(8,128)(2,1)}) %all-gather.5.cloned.1.call-update) | async-done | bytes 3145744 | tf_op jit(solution)/shard_map/all_gather | solution.py:127
  61.4 2.0 %fusion = f32[4,384,128,1]{2,1,0,3:T(8,128)S(1)} fusion(bf16[2,256,128,1]{2,1,3,0:T(8,128)(2,1)S(1)} %bitcast.35, bf16[2,8,256,384]{3,2,1,0:T(8,128)(2,1)} %bitcast.31, s32[]{:T(128)S(6)} %select_n.13), kind=kOutput, calls=%fused_computation.2 | convolution fusion | flops 201326592 | bytes 2490372 | tf_op jit(solution)/shard_map/szta,stb->zab/dot_general | solution.py:138
  63.4 0.1 fusion.2
  63.5 23.2 %all_to_all.15 = bf16[32,48,128]{2,1,0:T(8,128)(2,1)S(1)} all-to-all(bf16[32,48,128]{2,1,0:T(8,128)(2,1)S(1)} %bitcast.34), channel_id=1, replica_groups=mesh['y'=8,'x'=4,'core'=2,'z'=8] {'y','x'}, dimensions={0} | all-to-all | bytes 786432 | tf_op jit(solution)/shard_map/all_to_all | solution.py:140
  86.7 0.1 convert_reduce_fusion
  86.7 0.8 broadcast_in_dim.5
  87.6 4.8 %all-to-all-start.2 = ((bf16[32,48,128]{2,1,0:T(8,128)(2,1)}), bf16[32,48,128]{2,1,0:T(8,128)(2,1)S(1)}, u32[]{:S(2)}, u32[]{:S(2)}) async-start(bf16[32,48,128]{2,1,0:T(8,128)(2,1)} %broadcast_in_dim.5), calls=%async_computation.3 | async-start | bytes 786432 | tf_op jit(solution)/shard_map/all_to_all | solution.py:118
  92.3 1.6 %dynamic-slice_bitcast_fusion = bf16[8,384,256]{1,2,0:T(8,128)(2,1)S(1)} fusion(bf16[2,8,256,384]{3,2,1,0:T(8,128)(2,1)} %bitcast.32, s32[]{:T(128)S(6)} %select_n.16), kind=kLoop, calls=%fused_computation.1 | loop fusion | bytes 3145732 | tf_op jit(solution)/shard_map/zta,tb->zab/dot_general | solution.py:143
  93.9 1.6 %copy.13 = bf16[8,384,256]{2,1,0:T(8,128)(2,1)} copy(bf16[8,384,256]{1,2,0:T(8,128)(2,1)S(1)} %dynamic-slice_bitcast_fusion) | data formatting | bytes 3145728 | tf_op jit(solution)/shard_map/zta,tb->zab/dot_general | solution.py:143
  95.5 3.1 %convolution_add_fusion.merged_ref = f32[3072,128]{1,0:T(8,128)} fusion(f32[3072,128]{1,0:T(8,128)S(1)} %copy-done, bf16[3072,256]{1,0:T(8,128)(2,1)} %bitcast.29, bf16[256,128]{1,0:T(8,128)(2,1)} %out_grad_ref.1), kind=kOutput, calls=%fused_computation | convolution fusion | flops 201719808 | bytes 4784128 | tf_op jit(solution)/shard_map/zta,tb->zab/dot_general | solution.py:143
  98.7 6.5 %all-to-all-done.2 = bf16[32,48,128]{2,1,0:T(8,128)(2,1)S(1)} async-done(((bf16[32,48,128]{2,1,0:T(8,128)(2,1)}), bf16[32,48,128]{2,1,0:T(8,128)(2,1)S(1)}, u32[]{:S(2)}, u32[]{:S(2)}) %all-to-all-start.2) | async-done | bytes 393248 | tf_op jit(solution)/shard_map/all_to_all | solution.py:118
  105.2 5.5 %all_gather.27.mean_ref = bf16[3072,128]{1,0:T(8,128)(2,1)} all-gather(bf16[1536,128]{1,0:T(8,128)(2,1)S(1)} %bitcast.33), channel_id=1, replica_groups=mesh['y'=8,'x'=4,'core'=2,'z'=8] {'core'}, dimensions={0}, use_global_device_ids=true | all-gather | bytes 1179648 | tf_op jit(solution)/shard_map/all_gather | solution.py:148
  110.7 7.7 %basis_and_feedback.1 = (f32[3072,128]{1,0:T(8,128)}, f32[32,128]{1,0:T(8,128)}) custom-call(bf16[3072,128]{1,0:T(8,128)(2,1)} %all_gather.27.mean_ref, f32[3072,128]{1,0:T(8,128)} %convolution_add_fusion.merged_ref, f32[32,128]{1,0:T(8,128)} %bitcast.36), custom_call_target="tpu_custom_call" | custom-call | flops 301989888 | bytes 4000000 | tf_op jit(solution)/shard_map/basis_and_feedback/pallas_call | solution.py:97
  118.4 0.0 reduce-scatter.2.cloned.1.call-done
  (1 shorter events, 0.0 us)
Async XLA Ops:
  8.0 16.9 %copy-start.1 = (bf16[256,128]{1,0:T(8,128)(2,1)S(1)}, bf16[256,128]{1,0:T(8,128)(2,1)}, u32[]{:S(2)}) copy-start(bf16[256,128]{1,0:T(8,128)(2,1)} %out_grad_ref.1) | copy-start | bytes 196612
  8.0 53.4 %all-gather.5.cloned.1.call-start = ((), (), s32[]{:S(2)}) async-start(), calls=%async_computation.5 | async-start | bytes 3342336 | tf_op jit(solution)/shard_map/all_gather | solution.py:127
  10.2 24.3 %all-to-all-start = ((bf16[32,48,128]{2,1,0:T(8,128)(2,1)}), bf16[32,48,128]{2,1,0:T(8,128)(2,1)S(1)}, u32[]{:S(2)}, u32[]{:S(2)}) async-start(bf16[32,48,128]{2,1,0:T(8,128)(2,1)} %broadcast_in_dim.4), calls=%async_computation | async-start | bytes 786432 | tf_op jit(solution)/shard_map/all_to_all | solution.py:118
  20.8 97.7 %reduce-scatter.2.cloned.1.call-start = ((), (), s32[]{:S(2)}) async-start(), calls=%async_computation.4 | async-start | bytes 1769472 | tf_op jit(solution)/shard_map/reduce_scatter | solution.py:135
  22.0 23.4 %collective-permute-start = (f32[1536,128]{1,0:T(8,128)S(1)}, f32[1536,128]{1,0:T(8,128)S(1)}, u32[]{:S(2)}, u32[]{:S(2)}) collective-permute-start(f32[1536,128]{1,0:T(8,128)S(1)} %constant_dynamic-slice_fusion), channel_id=1, source_target_pairs={{0,8},{8,0},{1,9},{9,1},{2,10},{10,2},{3,11},{11,3},{4,12},{12,4},... | collective-permute-start | bytes 2359304 | tf_op jit(solution)/shard_map/ppermute | solution.py:122
  39.2 6.2 %copy-start = (f32[3072,128]{1,0:T(8,128)S(1)}, f32[3072,128]{1,0:T(8,128)}, u32[]{:S(2)}) copy-start(f32[3072,128]{1,0:T(8,128)} %param.8) | copy-start | bytes 4718596
  87.6 17.6 %all-to-all-start.2 = ((bf16[32,48,128]{2,1,0:T(8,128)(2,1)}), bf16[32,48,128]{2,1,0:T(8,128)(2,1)S(1)}, u32[]{:S(2)}, u32[]{:S(2)}) async-start(bf16[32,48,128]{2,1,0:T(8,128)(2,1)} %broadcast_in_dim.5), calls=%async_computation.3 | async-start | bytes 786432 | tf_op jit(solution)/shard_map/all_to_all | solution.py:118
Sparse Core Ops, SparseCore 0:
  11.0 50.3 all-gather.4
Sparse Core Ops, SparseCore 1:
  45.5 38.4 reduce-scatter.1

commit v3 on v2

v3 whole, which is shorter than its diff:
```python
import jax
import jax.numpy as jnp
from jax import lax
from jax.experimental import pallas as pl
from jax.experimental.pallas import tpu as pltpu
from jax.sharding import Mesh, PartitionSpec as P

BF = jnp.bfloat16
F32 = jnp.float32
HIGHEST = lax.Precision.HIGHEST
CHIPS = ("y", "x")
DP = ("y", "x", "core")
TENSOR = ("zh", "zl")
N_ZL = 4
N_CHIP = 32
REPLICAS = 64
D_IN = 3072
HALF = D_IN // 2
QUARTER = D_IN // 4
SLAB = D_IN // 8
PIECE = D_IN // REPLICAS
TOK = 256
COLS = 128
RANK = 32


def dot(a, b, dims, precision=None):
    return lax.dot_general(a, b, (dims, ((), ())), precision=precision, preferred_element_type=F32)


def tail_kernel(
    place_ref, mean_ref, own_ref, other_ref, warm_ref, pairs_ref, weight_ref,
    fresh_ref, right_ref, input_grad_ref,
    own_buf, other_buf, fresh_buf, pairs_buf, weight_buf, sems, out_sems,
):
    zh = place_ref[0]
    loads = [
        pltpu.make_async_copy(pairs_ref, pairs_buf, sems.at[0]),
        pltpu.make_async_copy(weight_ref, weight_buf, sems.at[1]),
        pltpu.make_async_copy(own_ref, own_buf, sems.at[2]),
        pltpu.make_async_copy(other_ref, other_buf, sems.at[3]),
    ]
    for load in loads:
        load.start()
    mean = mean_ref[...]
    warm = warm_ref[...]
    outer = dot(mean, mean, ((0,), (0,)))
    right = dot(warm, outer, ((1,), (0,)), HIGHEST)
    gram = dot(right, warm, ((1,), (1,)), HIGHEST)

    loads[0].wait()
    loads[1].wait()
    total = jnp.zeros((TOK, SLAB), F32)
    for half in range(2):
        start = pl.multiple_of((zh if half == 0 else 1 - zh) * COLS, COLS)
        for zl in range(N_ZL):
            grads = pairs_buf[zl, :, pl.ds(start, COLS)]
            block = (half * N_ZL + zl) * 4
            rows = [weight_buf[core, block + x] for x in range(4) for core in range(2)]
            total += dot(grads, jnp.concatenate(rows, axis=0), ((1,), (1,)))
    input_grad_ref[...] = total.astype(BF)

    row_at = lax.broadcasted_iota(jnp.int32, (RANK, 1), 0)
    for k in range(RANK):
        scale = lax.rsqrt(gram[k : k + 1, k : k + 1])
        column = jnp.where(row_at > k, gram[:, k : k + 1] * scale, 0.0)
        own = row_at == k
        gram_row = gram[k : k + 1] * scale
        right_row = right[k : k + 1] * scale
        warm_row = warm[k : k + 1] * scale
        gram = jnp.where(own, gram_row, gram - column * gram_row)
        right = jnp.where(own, right_row, right - column * right_row)
        warm = jnp.where(own, warm_row, warm - column * warm_row)
    right_ref[...] = right
    mix = dot(warm, right, ((0,), (0,)), HIGHEST)
    high = mix.astype(BF)
    low = (mix - high.astype(F32)).astype(BF)

    for load in loads[2:]:
        load.wait()
    stores = []
    for core in range(2):
        for side in range(2):
            at = core * 2 + side
            block = mean_ref[at * QUARTER : (at + 1) * QUARTER, :]
            approx = dot(block, high, ((1,), (0,))) + dot(block, low, ((1,), (0,)))
            merged = (own_buf, other_buf)[side][core * QUARTER : (core + 1) * QUARTER]
            fresh_buf[at] = merged - approx
            half = zh if side == 0 else 1 - zh
            start = pl.multiple_of(half * HALF + core * QUARTER, QUARTER)
            store = pltpu.make_async_copy(fresh_buf.at[at], fresh_ref.at[pl.ds(start, QUARTER)], out_sems.at[at])
            store.start()
            stores.append(store)
    for store in stores:
        store.wait()


def tail_call(place, mean, own_merged, other_merged, warm, pairs, weights):
    in_vmem = pl.BlockSpec(memory_space=pltpu.VMEM)
    in_hbm = pl.BlockSpec(memory_space=pl.ANY)
    return pl.pallas_call(
        tail_kernel,
        in_specs=[pl.BlockSpec(memory_space=pltpu.SMEM), in_vmem, in_hbm, in_hbm, in_vmem, in_hbm, in_hbm],
        out_specs=[in_hbm, in_vmem, in_vmem],
        out_shape=[
            jax.ShapeDtypeStruct((D_IN, COLS), F32),
            jax.ShapeDtypeStruct((RANK, COLS), F32),
            jax.ShapeDtypeStruct((TOK, SLAB), BF),
        ],
        scratch_shapes=[
            pltpu.VMEM((HALF, COLS), F32),
            pltpu.VMEM((HALF, COLS), F32),
            pltpu.VMEM((4, QUARTER, COLS), F32),
            pltpu.VMEM((N_ZL, TOK, 2 * COLS), BF),
            pltpu.VMEM((2, N_CHIP, PIECE, COLS), BF),
            pltpu.SemaphoreType.DMA((4,)),
            pltpu.SemaphoreType.DMA((4,)),
        ],
        compiler_params=pltpu.CompilerParams(vmem_limit_bytes=32 * 1024 * 1024),
        cost_estimate=pl.CostEstimate(flops=8 * COLS * COLS * D_IN, bytes_accessed=5000000, transcendentals=32),
        name="basis_feedback_input_grad",
    )(place, mean, own_merged, other_merged, warm, pairs, weights)


def swap_cores(block):
    return lax.ppermute(block, "core", [(0, 1), (1, 0)])


def swap_halves(block):
    return lax.ppermute(block, "zh", [(0, 1), (1, 0)])


def pick(block, at):
    return lax.dynamic_index_in_dim(block, at, 0, keepdims=False)


def to_all_chips(block):
    spread = lax.optimization_barrier(jnp.broadcast_to(block[None], (N_CHIP,) + block.shape))
    return lax.all_to_all(spread, CHIPS, 0, 0)


def on_device(features, out_grad, weight, feedback, warm_basis):
    core = lax.axis_index("core")
    zh = lax.axis_index("zh")
    barrier = lax.optimization_barrier

    partner_out_grad = swap_halves(out_grad)
    plane = [(i * 8 + j, j * 8 + i) for i in range(8) for j in range(8)]
    turned = lax.ppermute(weight, ("y",) + TENSOR, plane)

    gathered = lax.all_gather(features, "zl", axis=1, tiled=True)
    gathered, turned = barrier((gathered, turned))
    sent = dot(gathered, partner_out_grad, ((0,), (0,))).astype(BF)
    other_grads = swap_halves(sent)
    chip_weights = to_all_chips(turned)
    by_half = feedback.reshape(2, HALF, COLS)
    own_merged = dot(gathered, out_grad, ((0,), (0,))) + pick(by_half, zh)

    def chip_sum(rows):
        quarters = rows.reshape(2, QUARTER, COLS)
        other = swap_cores(pick(quarters, 1 - core).astype(BF))
        return (pick(quarters, core) + other.astype(F32)).astype(BF)

    own_sum = chip_sum(own_merged)
    other_merged = other_grads.astype(F32) + pick(by_half, 1 - zh)
    other_sum = chip_sum(other_merged)
    chips = jnp.concatenate([own_sum, other_sum], axis=0).reshape(N_CHIP, PIECE, COLS)

    chips, chip_weights, own_late, partner_late = barrier((chips, chip_weights, out_grad, partner_out_grad))
    parts = lax.all_to_all(chips, CHIPS, 0, 0)
    pairs = lax.all_gather(jnp.concatenate([own_late, partner_late], axis=1), "zl", axis=0)
    parts, pairs = barrier((parts, pairs))

    piece = (jnp.sum(parts.astype(F32), axis=0) / REPLICAS).astype(BF)
    piece, chip_weights = barrier((piece, chip_weights))
    weights = lax.all_gather(chip_weights, "core", axis=0)
    all_means = lax.all_gather(to_all_chips(piece), "core", axis=0).reshape(D_IN, COLS)
    place = zh.astype(jnp.int32).reshape(1)
    new_feedback, right, input_grad = tail_call(
        place, all_means, own_merged, other_merged, warm_basis.T, pairs, weights
    )
    return (input_grad, new_feedback, right.T)


def solution(mesh):
    grid = Mesh(mesh.devices.reshape(8, 4, 2, 2, 4), DP + TENSOR)
    return jax.shard_map(
        on_device,
        mesh=grid,
        in_specs=(P(DP, TENSOR), P(DP, TENSOR), P(DP, TENSOR), P(DP, TENSOR), P(TENSOR, None)),
        out_specs=(P(DP, TENSOR), P(DP, TENSOR), P(TENSOR, None)),
        check_vma=False,
    )
```

time: 127 us -> 124 us (0.976)
  starting transfers between devices: 18.2 us -> 61.2 us
  waiting for transfers between devices: 30.8 us -> 7.19 us
  between operations: 15.6 us -> 0.82 us
  Pallas kernels: 13.9 us -> 6.17 us
  blocking collectives: 35.3 us -> 41.7 us
  local copies, waits for them, and re-layouts: 6.75 us -> 1.7 us
  matrix products: 5.14 us -> 2.43 us
  other arithmetic: 0.24 us -> 2.03 us
    all_gather x3 -> x4, blocking collectives: 12.1 us -> 41.7 us  [the longest x1 15.4 us: on_device(): gathered = lax.all_gather(features, 'zl', axis=1, tiled=True)]
    all_to_all x1 -> x0, blocking collectives: 23.2 us -> none  [on_device(): parts = lax.all_to_all(chip_sum.reshape(N_CHIP, PIECE, COLS), CHIPS, 0, 0)]
    ppermute x0 -> x3, starting transfers between devices: none -> 20.3 us  [the longest x2 18.8 us: swap_halves(): return lax.ppermute(block, 'zh', [(0, 1), (1, 0)])]
    all_gather x1 -> x0, waiting for transfers between devices: 15.8 us -> none  [on_device(): lax.all_gather(features, ('core', 'z'), axis=0).reshape(2, N_Z, TOK, SLAB)]
    all_to_all x0 -> x1, starting transfers between devices: none -> 10.7 us  [on_device(): parts = lax.all_to_all(chips, CHIPS, 0, 0)]
    all_to_all x2, waiting for transfers between devices: 14.2 us -> 5.97 us  [to_all_chips(): return lax.all_to_all(spread, CHIPS, 0, 0)]
    pallas_call x2 -> x1, Pallas kernels: 13.9 us -> 6.17 us  [tail_call(): pl.pallas_call(tail_kernel, in_specs=[pl.BlockSpec(memory_space=pltpu.SME...]
    ppermute x1 -> x2, starting transfers between devices: 2.88 us -> 9.46 us  [swap_cores(): return lax.ppermute(block, 'core', [(0, 1), (1, 0)])]
  transfers between devices with their start and end apart: 5 -> 8, of which waited for: 3 -> 3; matrix products, arithmetic and copies ran while one was open for 10% -> 3% of each run, Pallas kernels for 11% -> 0%
where the time goes in v3:
time: 124 us; the launch traced here: 123 us
  starting transfers between devices  61.2 us (49%)
  blocking collectives  41.7 us (34%)
  waiting for transfers between devices  7.19 us (6%)
  Pallas kernels  6.17 us (5%)
  matrix products  2.43 us (2%)
  other arithmetic  2.03 us (2%)
  local copies, waits for them, and re-layouts  1.7 us (1%)
    all_to_all x2, starting transfers between devices, to_all_chips(): return lax.all_to_all(spread, CHIPS, 0, 0)  20.7 us
    ppermute x2, starting transfers between devices, swap_halves(): return lax.ppermute(block, 'zh', [(0, 1), (1, 0)])  18.8 us
    all_gather x1, blocking collectives, on_device(): gathered = lax.all_gather(features, 'zl', axis=1, tiled=True)  15.4 us
    all_gather x1, blocking collectives, on_device(): lax.all_gather(jnp.concatenate([own_late, partner_late], axis=1), 'zl', a...  13.6 us
    all_to_all x1, starting transfers between devices, on_device(): parts = lax.all_to_all(chips, CHIPS, 0, 0)  10.7 us
    ppermute x2, starting transfers between devices, swap_cores(): return lax.ppermute(block, 'core', [(0, 1), (1, 0)])  9.46 us
    all_gather x1, blocking collectives, on_device(): lax.all_gather(to_all_chips(piece), 'core', axis=0).reshape(D_IN, COLS)  7.19 us
    pallas_call x1, Pallas kernels, tail_call(): pl.pallas_call(tail_kernel, in_specs=[pl.BlockSpec(memory_space=pltpu.SME...  6.17 us
  transfers between devices with their start and end apart: 8, of which 3 were waited for; matrix products, arithmetic and copies ran while one was open for 3% of the time, Pallas kernels for 0%

profile of v3, /device:TPU:1, one launch (start us, length us, event | category | flops | bytes accessed | tf_op | source)
XLA Modules:
  0.0 123.2 jit_solution(11081515198706223404)
XLA Ops:
  0.6 0.0 copy-start.1
  0.6 1.5 %collective-permute-start = (bf16[48,128]{1,0:T(8,128)(2,1)}, bf16[48,128]{1,0:T(8,128)(2,1)S(1)}, u32[]{:S(2)}, u32[]{:S(2)}) collective-permute-start(bf16[48,128]{1,0:T(8,128)(2,1)} %param.7), channel_id=1, source_target_pairs={{0,0},{1,64},{2,128},{3,192},{4,256},{5,320},{6,384},{7,448},{64,1... | collective-permute-start | bytes 36872 | tf_op jit(solution)/shard_map/ppermute | solution.py:149
  2.1 13.9 %collective-permute-start.2 = (bf16[256,128]{1,0:T(8,128)(2,1)}, bf16[256,128]{1,0:T(8,128)(2,1)S(1)}, u32[]{:S(2)}, u32[]{:S(2)}) collective-permute-start(bf16[256,128]{1,0:T(8,128)(2,1)} %param.6), channel_id=1, source_target_pairs={{0,4},{4,0},{1,5},{5,1},{2,6},{6,2},{3,7},{7,3},{8,12},{12,8},{9,1... | collective-permute-start | bytes 196616 | tf_op jit(solution)/shard_map/ppermute | solution.py:130
  16.1 15.4 %all_gather.21 = bf16[256,1536]{1,0:T(8,128)(2,1)S(1)} all-gather(bf16[256,384]{1,0:T(8,128)(2,1)} %param.5), channel_id=1, replica_groups=mesh['y'=8,'x'=4,'core'=2,'zh'=2,'zl'=4] {'zl'}, dimensions={1}, use_global_device_ids=true | all-gather | bytes 983040 | tf_op jit(solution)/shard_map/all_gather | solution.py:151
  31.5 0.0 collective-permute-done
  31.5 0.0 collective-permute-done.2
  31.5 0.0 copy-start.2
  31.5 1.2 convolution_convert_fusion
  32.7 4.9 %collective-permute-start.3 = (bf16[1536,128]{1,0:T(8,128)(2,1)}, bf16[1536,128]{1,0:T(8,128)(2,1)}, u32[]{:S(2)}, u32[]{:S(2)}) collective-permute-start(bf16[1536,128]{1,0:T(8,128)(2,1)} %convolution_convert_fusion), channel_id=1, source_target_pairs={{0,4},{4,0},{1,5},{5,1},{2,6},{6,2},{3,7},{7,3},{8,12},{12,8},{9,1... | collective-permute-start | bytes 1179656 | tf_op jit(solution)/shard_map/ppermute | solution.py:130
  37.6 0.8 broadcast_in_dim.4
  38.4 11.7 %all-to-all-start = ((bf16[32,48,128]{2,1,0:T(8,128)(2,1)}), bf16[32,48,128]{2,1,0:T(8,128)(2,1)S(1)}, u32[]{:S(2)}, u32[]{:S(2)}) async-start(bf16[32,48,128]{2,1,0:T(8,128)(2,1)} %broadcast_in_dim.4), calls=%async_computation | async-start | bytes 786432 | tf_op jit(solution)/shard_map/all_to_all | solution.py:139
  50.2 0.0 copy-done.2
  50.2 0.0 copy-done.1
  50.2 1.3 %convolution_add_fusion.own_ref = f32[1536,128]{1,0:T(8,128)S(1)} fusion(bf16[256,1536]{1,0:T(8,128)(2,1)S(1)} %all_gather.21, bf16[256,128]{1,0:T(8,128)(2,1)} %param.6, f32[2,1536,128]{2,1,0:T(8,128)S(1)} %bitcast.38, s32[]{:T(128)S(6)} %select_n.16), kind=kOutput, calls=%fused_computation | convolution fusion | flops 100859904 | bytes 2424836 | tf_op jit(solution)/shard_map/dot_general | solution.py:28
  51.5 6.4 %collective-permute-start.1 = (bf16[768,128]{1,0:T(8,128)(2,1)S(1)}, bf16[768,128]{1,0:T(8,128)(2,1)S(1)}, u32[]{:S(2)}, u32[]{:S(2)}) collective-permute-start(bf16[768,128]{1,0:T(8,128)(2,1)S(1)} %fusion.2), channel_id=1, source_target_pairs={{0,8},{8,0},{1,9},{9,1},{2,10},{10,2},{3,11},{11,3},{4,12},{12,4},... | collective-permute-start | bytes 589832 | tf_op jit(solution)/shard_map/ppermute | solution.py:126
  57.9 0.0 collective-permute-done.3
  57.9 1.1 bitcast_add_fusion.other_ref
  59.1 0.0 copy-start.3
  59.1 0.0 copy-start.4
  59.1 3.0 %collective-permute-start.4 = (bf16[768,128]{1,0:T(8,128)(2,1)S(1)}, bf16[768,128]{1,0:T(8,128)(2,1)S(1)}, u32[]{:S(2)}, u32[]{:S(2)}) collective-permute-start(bf16[768,128]{1,0:T(8,128)(2,1)S(1)} %fusion.3), channel_id=1, source_target_pairs={{0,8},{8,0},{1,9},{9,1},{2,10},{10,2},{3,11},{11,3},{4,12},{12,4},... | collective-permute-start | bytes 589832 | tf_op jit(solution)/shard_map/ppermute | solution.py:126
  62.1 0.0 collective-permute-done.1
  62.2 1.0 collective-permute-done.4
  63.2 0.8 pad_maximum_fusion
  64.0 0.0 all-to-all-done
  64.0 10.7 %all-to-all-start.1 = ((bf16[32,48,128]{2,1,0:T(8,128)(2,1)}), bf16[32,48,128]{2,1,0:T(8,128)(2,1)S(1)}, u32[]{:S(2)}, u32[]{:S(2)}) async-start(bf16[32,48,128]{2,1,0:T(8,128)(2,1)} %bitcast.10), calls=%async_computation.1 | async-start | bytes 786432 | tf_op jit(solution)/shard_map/all_to_all | solution.py:170
  74.7 0.0 copy-done.3
  74.7 0.0 copy-done.4
  74.7 13.6 %all-gather = bf16[1024,256]{1,0:T(8,128)(2,1)S(1)} all-gather(bf16[256,256]{1,0:T(8,128)(2,1)S(1)} %pad_maximum_fusion.1), channel_id=2, replica_groups=mesh['y'=8,'x'=4,'core'=2,'zh'=2,'zl'=4] {'zl'}, dimensions={0}, use_global_device_ids=true | all-gather | bytes 655360 | tf_op jit(solution)/shard_map/all_gather | solution.py:171
  88.3 0.2 all-to-all-done.1
  88.6 0.1 convert_reduce_fusion
  88.6 0.8 broadcast_in_dim.5
  89.4 0.0 copy-start
  89.4 8.9 %all-to-all-start.2 = ((bf16[32,48,128]{2,1,0:T(8,128)(2,1)}), bf16[32,48,128]{2,1,0:T(8,128)(2,1)}, u32[]{:S(2)}, u32[]{:S(2)}) async-start(bf16[32,48,128]{2,1,0:T(8,128)(2,1)} %broadcast_in_dim.5), calls=%async_computation.2 | async-start | bytes 786432 | tf_op jit(solution)/shard_map/all_to_all | solution.py:139
  98.4 5.5 %all-gather.2 = bf16[64,48,128]{2,1,0:T(8,128)(2,1)S(1)} all-gather(bf16[32,48,128]{2,1,0:T(8,128)(2,1)S(1)} %all-to-all-done), channel_id=4, replica_groups=mesh['y'=8,'x'=4,'core'=2,'zh'=2,'zl'=4] {'core'}, dimensions={0}, use_global_device_ids=true | all-gather | bytes 1179648 | tf_op jit(solution)/shard_map/all_gather | solution.py:176
  103.9 6.0 %all-to-all-done.2 = bf16[32,48,128]{2,1,0:T(8,128)(2,1)} async-done(((bf16[32,48,128]{2,1,0:T(8,128)(2,1)}), bf16[32,48,128]{2,1,0:T(8,128)(2,1)}, u32[]{:S(2)}, u32[]{:S(2)}) %all-to-all-start.2) | async-done | bytes 393248 | tf_op jit(solution)/shard_map/all_to_all | solution.py:139
  109.9 7.2 %all-gather.1 = bf16[64,48,128]{2,1,0:T(8,128)(2,1)S(1)} all-gather(bf16[32,48,128]{2,1,0:T(8,128)(2,1)} %all-to-all-done.2), channel_id=3, replica_groups=mesh['y'=8,'x'=4,'core'=2,'zh'=2,'zl'=4] {'core'}, dimensions={0}, use_global_device_ids=true | all-gather | bytes 1179648 | tf_op jit(solution)/shard_map/all_gather | solution.py:177
  117.0 0.0 copy-done
  117.1 6.2 %basis_feedback_input_grad.1 = (f32[3072,128]{1,0:T(8,128)}, f32[32,128]{1,0:T(8,128)}, bf16[256,384]{1,0:T(8,128)(2,1)}) custom-call(s32[1]{0:T(128)} %bitcast.place_ref, bf16[3072,128]{1,0:T(8,128)(2,1)S(1)} %bitcast.35, f32[1536,128]{1,0:T(8,128)S(1)} %convolution_add_fusion.own_ref, f32[1536,128]{1,0:T(8,128)S(1)} %bitcast_add_fusion.other_ref, ...), custom_call_target="tpu_custom_call" | custom-call | flops 402653184 | bytes 5000000 | tf_op jit(solution)/shard_map/basis_feedback_input_grad/pallas_call | solution.py:101
  (6 shorter events, 0.2 us)
Async XLA Ops:
  0.6 49.6 %copy-start.1 = (f32[3072,128]{1,0:T(8,128)S(1)}, f32[3072,128]{1,0:T(8,128)}, u32[]{:S(2)}) copy-start(f32[3072,128]{1,0:T(8,128)} %param.8) | copy-start | bytes 4718596
  0.6 30.9 %collective-permute-start = (bf16[48,128]{1,0:T(8,128)(2,1)}, bf16[48,128]{1,0:T(8,128)(2,1)S(1)}, u32[]{:S(2)}, u32[]{:S(2)}) collective-permute-start(bf16[48,128]{1,0:T(8,128)(2,1)} %param.7), channel_id=1, source_target_pairs={{0,0},{1,64},{2,128},{3,192},{4,256},{5,320},{6,384},{7,448},{64,1... | collective-permute-start | bytes 36872 | tf_op jit(solution)/shard_map/ppermute | solution.py:149
  2.1 29.4 %collective-permute-start.2 = (bf16[256,128]{1,0:T(8,128)(2,1)}, bf16[256,128]{1,0:T(8,128)(2,1)S(1)}, u32[]{:S(2)}, u32[]{:S(2)}) collective-permute-start(bf16[256,128]{1,0:T(8,128)(2,1)} %param.6), channel_id=1, source_target_pairs={{0,4},{4,0},{1,5},{5,1},{2,6},{6,2},{3,7},{7,3},{8,12},{12,8},{9,1... | collective-permute-start | bytes 196616 | tf_op jit(solution)/shard_map/ppermute | solution.py:130
  31.5 18.6 %copy-start.2 = (bf16[256,128]{1,0:T(8,128)(2,1)}, bf16[256,128]{1,0:T(8,128)(2,1)S(1)}, u32[]{:S(2)}) copy-start(bf16[256,128]{1,0:T(8,128)(2,1)S(1)} %collective-permute-done.2) | copy-start | bytes 196612
  32.7 25.2 %collective-permute-start.3 = (bf16[1536,128]{1,0:T(8,128)(2,1)}, bf16[1536,128]{1,0:T(8,128)(2,1)}, u32[]{:S(2)}, u32[]{:S(2)}) collective-permute-start(bf16[1536,128]{1,0:T(8,128)(2,1)} %convolution_convert_fusion), channel_id=1, source_target_pairs={{0,4},{4,0},{1,5},{5,1},{2,6},{6,2},{3,7},{7,3},{8,12},{12,8},{9,1... | collective-permute-start | bytes 1179656 | tf_op jit(solution)/shard_map/ppermute | solution.py:130
  38.4 25.5 %all-to-all-start = ((bf16[32,48,128]{2,1,0:T(8,128)(2,1)}), bf16[32,48,128]{2,1,0:T(8,128)(2,1)S(1)}, u32[]{:S(2)}, u32[]{:S(2)}) async-start(bf16[32,48,128]{2,1,0:T(8,128)(2,1)} %broadcast_in_dim.4), calls=%async_computation | async-start | bytes 786432 | tf_op jit(solution)/shard_map/all_to_all | solution.py:139
  51.5 10.6 %collective-permute-start.1 = (bf16[768,128]{1,0:T(8,128)(2,1)S(1)}, bf16[768,128]{1,0:T(8,128)(2,1)S(1)}, u32[]{:S(2)}, u32[]{:S(2)}) collective-permute-start(bf16[768,128]{1,0:T(8,128)(2,1)S(1)} %fusion.2), channel_id=1, source_target_pairs={{0,8},{8,0},{1,9},{9,1},{2,10},{10,2},{3,11},{11,3},{4,12},{12,4},... | collective-permute-start | bytes 589832 | tf_op jit(solution)/shard_map/ppermute | solution.py:126
  59.1 15.6 %copy-start.3 = (bf16[256,128]{1,0:T(8,128)(2,1)S(1)}, bf16[256,128]{1,0:T(8,128)(2,1)}, u32[]{:S(2)}) copy-start(bf16[256,128]{1,0:T(8,128)(2,1)} %copy-done.2) | copy-start | bytes 196612
  59.1 15.6 %copy-start.4 = (bf16[256,128]{1,0:T(8,128)(2,1)S(1)}, bf16[256,128]{1,0:T(8,128)(2,1)}, u32[]{:S(2)}) copy-start(bf16[256,128]{1,0:T(8,128)(2,1)} %param.6) | copy-start | bytes 196612
  59.1 4.1 %collective-permute-start.4 = (bf16[768,128]{1,0:T(8,128)(2,1)S(1)}, bf16[768,128]{1,0:T(8,128)(2,1)S(1)}, u32[]{:S(2)}, u32[]{:S(2)}) collective-permute-start(bf16[768,128]{1,0:T(8,128)(2,1)S(1)} %fusion.3), channel_id=1, source_target_pairs={{0,8},{8,0},{1,9},{9,1},{2,10},{10,2},{3,11},{11,3},{4,12},{12,4},... | collective-permute-start | bytes 589832 | tf_op jit(solution)/shard_map/ppermute | solution.py:126
  64.0 24.6 %all-to-all-start.1 = ((bf16[32,48,128]{2,1,0:T(8,128)(2,1)}), bf16[32,48,128]{2,1,0:T(8,128)(2,1)S(1)}, u32[]{:S(2)}, u32[]{:S(2)}) async-start(bf16[32,48,128]{2,1,0:T(8,128)(2,1)} %bitcast.10), calls=%async_computation.1 | async-start | bytes 786432 | tf_op jit(solution)/shard_map/all_to_all | solution.py:170
  89.4 27.6 %copy-start = (f32[128,32]{0,1:T(8,128)S(1)}, f32[128,32]{0,1:T(8,128)}, u32[]{:S(2)}) copy-start(f32[128,32]{0,1:T(8,128)} %param.9) | copy-start | bytes 49156
  89.4 20.4 %all-to-all-start.2 = ((bf16[32,48,128]{2,1,0:T(8,128)(2,1)}), bf16[32,48,128]{2,1,0:T(8,128)(2,1)}, u32[]{:S(2)}, u32[]{:S(2)}) async-start(bf16[32,48,128]{2,1,0:T(8,128)(2,1)} %broadcast_in_dim.5), calls=%async_computation.2 | async-start | bytes 786432 | tf_op jit(solution)/shard_map/all_to_all | solution.py:139

commit v4 on v3

v4 whole, which is shorter than its diff:
```python
import jax
import jax.numpy as jnp
from jax import lax
from jax.experimental import pallas as pl
from jax.experimental.pallas import tpu as pltpu
from jax.sharding import Mesh, PartitionSpec as P

BF = jnp.bfloat16
F32 = jnp.float32
HIGHEST = lax.Precision.HIGHEST
CHIPS = ("y", "x")
DP = ("y", "x", "core")
TENSOR = ("zl", "zh")
N_ZL = 4
N_CHIP = 32
REPLICAS = 64
D_IN = 3072
HALF = D_IN // 2
QUARTER = D_IN // 4
SLAB = D_IN // 8
PIECE = D_IN // REPLICAS
TOK = 256
COLS = 128
RANK = 32


def dot(a, b, dims, precision=None):
    return lax.dot_general(a, b, (dims, ((), ())), precision=precision, preferred_element_type=F32)


def tail_kernel(
    place_ref, mean_ref, own_ref, other_ref, warm_ref, near_ref, far_ref, weight_ref,
    fresh_ref, right_ref, input_grad_ref,
    own_buf, other_buf, fresh_buf, out_grad_buf, weight_buf, sems, out_sems,
):
    zh = place_ref[0]
    loads = [
        pltpu.make_async_copy(near_ref, out_grad_buf.at[0], sems.at[0]),
        pltpu.make_async_copy(far_ref, out_grad_buf.at[1], sems.at[1]),
        pltpu.make_async_copy(weight_ref, weight_buf, sems.at[2]),
        pltpu.make_async_copy(own_ref, own_buf, sems.at[3]),
        pltpu.make_async_copy(other_ref, other_buf, sems.at[4]),
    ]
    for load in loads:
        load.start()
    mean = mean_ref[...]
    warm = warm_ref[...]
    outer = dot(mean, mean, ((0,), (0,)))
    right = dot(warm, outer, ((1,), (0,)), HIGHEST)
    gram = dot(right, warm, ((1,), (1,)), HIGHEST)

    for load in loads[:3]:
        load.wait()
    total = jnp.zeros((TOK, SLAB), F32)
    for half in range(2):
        side = zh if half == 0 else 1 - zh
        for zl in range(N_ZL):
            grads = out_grad_buf[side, zl]
            block = (zl * 2 + half) * 4
            rows = [weight_buf[core, block + x] for x in range(4) for core in range(2)]
            total += dot(grads, jnp.concatenate(rows, axis=0), ((1,), (1,)))
    input_grad_ref[...] = total.astype(BF)

    row_at = lax.broadcasted_iota(jnp.int32, (RANK, 1), 0)
    for k in range(RANK):
        scale = lax.rsqrt(gram[k : k + 1, k : k + 1])
        column = jnp.where(row_at > k, gram[:, k : k + 1] * scale, 0.0)
        own = row_at == k
        gram_row = gram[k : k + 1] * scale
        right_row = right[k : k + 1] * scale
        warm_row = warm[k : k + 1] * scale
        gram = jnp.where(own, gram_row, gram - column * gram_row)
        right = jnp.where(own, right_row, right - column * right_row)
        warm = jnp.where(own, warm_row, warm - column * warm_row)
    right_ref[...] = right
    mix = dot(warm, right, ((0,), (0,)), HIGHEST)
    high = mix.astype(BF)
    low = (mix - high.astype(F32)).astype(BF)

    for load in loads[3:]:
        load.wait()
    stores = []
    for core in range(2):
        for side in range(2):
            at = core * 2 + side
            block = mean_ref[at * QUARTER : (at + 1) * QUARTER, :]
            approx = dot(block, high, ((1,), (0,))) + dot(block, low, ((1,), (0,)))
            merged = (own_buf, other_buf)[side][core * QUARTER : (core + 1) * QUARTER]
            fresh_buf[at] = merged - approx
            half = zh if side == 0 else 1 - zh
            for slab in range(2):
                start = pl.multiple_of(((core * 2 + slab) * 2 + half) * SLAB, SLAB)
                store = pltpu.make_async_copy(
                    fresh_buf.at[at, pl.ds(slab * SLAB, SLAB)],
                    fresh_ref.at[pl.ds(start, SLAB)],
                    out_sems.at[at, slab],
                )
                store.start()
                stores.append(store)
    for store in stores:
        store.wait()


def tail_call(place, mean, own_merged, other_merged, warm, near, far, weights):
    in_vmem = pl.BlockSpec(memory_space=pltpu.VMEM)
    in_hbm = pl.BlockSpec(memory_space=pl.ANY)
    return pl.pallas_call(
        tail_kernel,
        in_specs=[pl.BlockSpec(memory_space=pltpu.SMEM), in_vmem, in_hbm, in_hbm, in_vmem] + [in_hbm] * 3,
        out_specs=[in_hbm, in_vmem, in_vmem],
        out_shape=[
            jax.ShapeDtypeStruct((D_IN, COLS), F32),
            jax.ShapeDtypeStruct((RANK, COLS), F32),
            jax.ShapeDtypeStruct((TOK, SLAB), BF),
        ],
        scratch_shapes=[
            pltpu.VMEM((HALF, COLS), F32),
            pltpu.VMEM((HALF, COLS), F32),
            pltpu.VMEM((4, QUARTER, COLS), F32),
            pltpu.VMEM((2, N_ZL, TOK, COLS), BF),
            pltpu.VMEM((2, N_CHIP, PIECE, COLS), BF),
            pltpu.SemaphoreType.DMA((5,)),
            pltpu.SemaphoreType.DMA((4, 2)),
        ],
        compiler_params=pltpu.CompilerParams(vmem_limit_bytes=32 * 1024 * 1024),
        cost_estimate=pl.CostEstimate(flops=8 * COLS * COLS * D_IN, bytes_accessed=5000000, transcendentals=32),
        name="basis_feedback_input_grad",
    )(place, mean, own_merged, other_merged, warm, near, far, weights)


def swap_halves(block):
    return lax.ppermute(block, "zh", [(0, 1), (1, 0)])


def pick(block, at):
    return lax.dynamic_index_in_dim(block, at, 0, keepdims=False)


def to_all_chips(block):
    spread = lax.optimization_barrier(jnp.broadcast_to(block[None], (N_CHIP,) + block.shape))
    return lax.all_to_all(spread, CHIPS, 0, 0)


def on_device(features, out_grad, weight, feedback, warm_basis):
    core = lax.axis_index("core")
    zh = lax.axis_index("zh")
    barrier = lax.optimization_barrier

    partner_out_grad = swap_halves(out_grad)
    plane = [(i * 8 + j, j * 8 + i) for i in range(8) for j in range(8)]
    turned = lax.ppermute(weight, ("y",) + TENSOR, plane)

    gathered = lax.all_gather(features, "zl", axis=1, tiled=True)
    gathered, turned = barrier((gathered, turned))
    sent = dot(gathered, partner_out_grad, ((0,), (0,))).astype(BF)
    other_grads = swap_halves(sent)
    chip_weights = to_all_chips(turned)
    slabs = feedback.reshape(N_ZL, 2, SLAB, COLS)

    def add_feedback(grads, half):
        own = lax.dynamic_slice(slabs, (0, half, 0, 0), (N_ZL, 1, SLAB, COLS))
        return (grads.reshape(own.shape).astype(F32) + own).reshape(HALF, COLS)

    own_merged = add_feedback(dot(gathered, out_grad, ((0,), (0,))), zh)

    other_merged = add_feedback(other_grads, 1 - zh)

    def quarters(at):
        return jnp.stack([pick(rows.reshape(2, QUARTER, COLS), at) for rows in (own_merged, other_merged)])

    swapped = lax.all_gather(quarters(1 - core).astype(BF), "core", axis=0)
    chips = (quarters(core) + pick(swapped, 1 - core).astype(F32)).astype(BF).reshape(N_CHIP, PIECE, COLS)

    chips, chip_weights, late = barrier((chips, chip_weights, out_grad))
    parts = lax.all_to_all(chips, CHIPS, 0, 0)
    near = lax.all_gather(late, "zl", axis=0)
    parts, near = barrier((parts, near))

    piece = (jnp.sum(parts.astype(F32), axis=0) / REPLICAS).astype(BF)
    piece, chip_weights, near = barrier((piece, chip_weights, near))
    far = swap_halves(near)
    weights = lax.all_gather(chip_weights, "core", axis=0)
    all_means = lax.all_gather(to_all_chips(piece), "core", axis=0).reshape(D_IN, COLS)
    place = zh.astype(jnp.int32).reshape(1)
    new_feedback, right, input_grad = tail_call(
        place, all_means, own_merged, other_merged, warm_basis.T, near, far, weights
    )
    return (input_grad, new_feedback, right.T)


def solution(mesh):
    grid = Mesh(mesh.devices.reshape(8, 4, 2, 4, 2), DP + TENSOR)
    return jax.shard_map(
        on_device,
        mesh=grid,
        in_specs=(P(DP, TENSOR), P(DP, TENSOR), P(DP, TENSOR), P(DP, TENSOR), P(TENSOR, None)),
        out_specs=(P(DP, TENSOR), P(DP, TENSOR), P(TENSOR, None)),
        check_vma=False,
    )
```

time: 124 us -> 117 us (0.944)
  starting transfers between devices: 61.2 us -> 41.8 us
  blocking collectives: 41.7 us -> 56.9 us
  waiting for transfers between devices: 7.19 us -> 4.72 us
    all_gather x1, blocking collectives: 15.4 us -> 25.6 us  [on_device(): gathered = lax.all_gather(features, 'zl', axis=1, tiled=True)]
    ppermute x2 -> x0, starting transfers between devices: 9.46 us -> none  [swap_cores(): return lax.ppermute(block, 'core', [(0, 1), (1, 0)])]
    ppermute x2 -> x3, starting transfers between devices: 18.8 us -> 13.2 us  [swap_halves(): return lax.ppermute(block, 'zh', [(0, 1), (1, 0)])]
    all_gather x1 -> x2, blocking collectives: 13.6 us -> 18 us  [the longest x1 12.3 us: on_device(): near = lax.all_gather(late, 'zl', axis=0)]
    all_to_all x2, waiting for transfers between devices: 5.97 us -> 3.15 us  [to_all_chips(): return lax.all_to_all(spread, CHIPS, 0, 0)]
    all_to_all x1, starting transfers between devices: 10.7 us -> 7.97 us  [on_device(): parts = lax.all_to_all(chips, CHIPS, 0, 0)]
    all_to_all x2, starting transfers between devices: 20.7 us -> 19.2 us  [to_all_chips(): return lax.all_to_all(spread, CHIPS, 0, 0)]
    all_to_all x1, waiting for transfers between devices: 0.23 us -> 1.56 us  [on_device(): parts = lax.all_to_all(chips, CHIPS, 0, 0)]
  transfers between devices with their start and end apart: 8 -> 7, of which waited for: 3 -> 3; matrix products, arithmetic and copies ran while one was open for 3% -> 4% of each run, Pallas kernels for 0% -> 0%
where the time goes in v4:
time: 117 us
  blocking collectives  56.9 us (49%)
  starting transfers between devices  41.8 us (36%)
  Pallas kernels  6.21 us (5%)
  waiting for transfers between devices  4.72 us (4%)
  local copies, waits for them, and re-layouts  2.5 us (2%)
  other arithmetic  2.18 us (2%)
  matrix products  1.67 us (1%)
    all_gather x1, blocking collectives, on_device(): gathered = lax.all_gather(features, 'zl', axis=1, tiled=True)  25.6 us
    all_to_all x2, starting transfers between devices, to_all_chips(): return lax.all_to_all(spread, CHIPS, 0, 0)  19.2 us
    ppermute x3, starting transfers between devices, swap_halves(): return lax.ppermute(block, 'zh', [(0, 1), (1, 0)])  13.2 us
    all_gather x1, blocking collectives, on_device(): near = lax.all_gather(late, 'zl', axis=0)  12.3 us
    all_to_all x1, starting transfers between devices, on_device(): parts = lax.all_to_all(chips, CHIPS, 0, 0)  7.97 us
    all_gather x1, blocking collectives, on_device(): lax.all_gather(to_all_chips(piece), 'core', axis=0).reshape(D_IN, COLS)  7.25 us
    pallas_call x1, Pallas kernels, tail_call(): pl.pallas_call(tail_kernel, in_specs=[pl.BlockSpec(memory_space=pltpu.SME...  6.21 us
    all_gather x1, blocking collectives, on_device(): weights = lax.all_gather(chip_weights, 'core', axis=0)  6.02 us
  transfers between devices with their start and end apart: 7, of which 3 were waited for; matrix products, arithmetic and copies ran while one was open for 4% of the time, Pallas kernels for 0%

profile of v4, /device:TPU:1, one launch (start us, length us, event | category | flops | bytes accessed | tf_op | source)
XLA Modules:
  0.0 116.7 jit_solution(10568456605389624468)
XLA Ops:
  0.6 1.4 %collective-permute-start = (bf16[48,128]{1,0:T(8,128)(2,1)}, bf16[48,128]{1,0:T(8,128)(2,1)S(1)}, u32[]{:S(2)}, u32[]{:S(2)}) collective-permute-start(bf16[48,128]{1,0:T(8,128)(2,1)} %param.7), channel_id=1, source_target_pairs={{0,0},{1,64},{2,128},{3,192},{4,256},{5,320},{6,384},{7,448},{64,1... | collective-permute-start | bytes 36872 | tf_op jit(solution)/shard_map/ppermute | solution.py:151
  2.0 5.8 %collective-permute-start.1 = (bf16[256,128]{1,0:T(8,128)(2,1)}, bf16[256,128]{1,0:T(8,128)(2,1)S(1)}, u32[]{:S(2)}, u32[]{:S(2)}) collective-permute-start(bf16[256,128]{1,0:T(8,128)(2,1)} %param.6), channel_id=1, source_target_pairs={{0,1},{1,0},{2,3},{3,2},{4,5},{5,4},{6,7},{7,6},{8,9},{9,8},{10,11... | collective-permute-start | bytes 196616 | tf_op jit(solution)/shard_map/ppermute | solution.py:132
  7.8 25.6 %all_gather.25 = bf16[256,1536]{1,0:T(8,128)(2,1)S(1)} all-gather(bf16[256,384]{1,0:T(8,128)(2,1)} %param.5), channel_id=1, replica_groups=mesh['y'=8,'x'=4,'core'=2,'zl'=4,'zh'=2] {'zl'}, dimensions={1}, use_global_device_ids=true | all-gather | bytes 983040 | tf_op jit(solution)/shard_map/all_gather | solution.py:153
  33.3 0.0 collective-permute-done
  33.3 0.0 collective-permute-done.1
  33.4 0.4 convolution_convert_fusion
  33.8 0.0 copy-start.1
  33.8 3.5 %collective-permute-start.2 = (bf16[1536,128]{1,0:T(8,128)(2,1)S(1)}, bf16[1536,128]{1,0:T(8,128)(2,1)S(1)}, u32[]{:S(2)}, u32[]{:S(2)}) collective-permute-start(bf16[1536,128]{1,0:T(8,128)(2,1)S(1)} %convolution_convert_fusion), channel_id=1, source_target_pairs={{0,1},{1,0},{2,3},{3,2},{4,5},{5,4},{6,7},{7,6},{8,9},{9,8},{10,11... | collective-permute-start | bytes 1179656 | tf_op jit(solution)/shard_map/ppermute | solution.py:132
  37.3 0.8 broadcast_in_dim.4
  38.1 11.6 %all-to-all-start = ((bf16[32,48,128]{2,1,0:T(8,128)(2,1)}), bf16[32,48,128]{2,1,0:T(8,128)(2,1)S(1)}, u32[]{:S(2)}, u32[]{:S(2)}) async-start(bf16[32,48,128]{2,1,0:T(8,128)(2,1)} %broadcast_in_dim.4), calls=%async_computation | async-start | bytes 786432 | tf_op jit(solution)/shard_map/all_to_all | solution.py:141
  49.7 1.3 %fusion.3 = f32[1536,128]{1,0:T(8,128)S(1)} fusion(bf16[256,1536]{1,0:T(8,128)(2,1)S(1)} %all_gather.25, bf16[256,128]{1,0:T(8,128)(2,1)} %param.6), kind=kOutput, calls=%fused_computation.16 | convolution fusion | flops 100663296 | bytes 1638400 | tf_op jit(solution)/shard_map/dot_general | solution.py:28
  51.0 0.0 collective-permute-done.2
  51.0 0.0 copy-start.2
  51.0 0.7 copy-done.2
  51.7 0.0 copy-done.1
  51.7 1.2 %bitcast_add_fusion.1 = (f32[4,1,384,128]{3,2,0,1:T(8,128)S(1)}, f32[4,1,384,128]{3,2,0,1:T(8,128)S(1)}) fusion(f32[4,1,384,128]{3,2,0,1:T(8,128)S(1)} %bitcast.40, f32[4,2,384,128]{3,2,1,0:T(8,128)S(1)} %bitcast.42, s32[]{:T(128)S(6)} %select_n.17, s32[]{:T(128)S(6)} %select_n.19, bf16[4,1,384,128]{3,2,0,1:T(8,128)(2,1)} %bitcast.44), kind=kLoop, calls=%fused_computation.3 | loop fusion | flops 589824 | bytes 4325384 | tf_op jit(solution)/shard_map/add | solution.py:162
  52.9 0.1 fusion.1
  53.0 5.7 %all_gather.26 = bf16[2,2,768,128]{3,2,1,0:T(8,128)(2,1)S(1)} all-gather(bf16[1,2,768,128]{3,2,1,0:T(8,128)(2,1)S(1)} %pad_maximum_fusion.1), channel_id=1, replica_groups=mesh['y'=8,'x'=4,'core'=2,'zl'=4,'zh'=2] {'core'}, dimensions={0}, use_global_device_ids=true | all-gather | bytes 1179648 | tf_op jit(solution)/shard_map/all_gather | solution.py:171
  58.7 0.1 constant_dynamic-slice_fusion.1
  58.8 0.1 pad_maximum_fusion
  58.9 0.0 copy-start.3
  58.9 0.8 fusion
  59.7 1.5 %all-to-all-done = bf16[32,48,128]{2,1,0:T(8,128)(2,1)S(1)} async-done(((bf16[32,48,128]{2,1,0:T(8,128)(2,1)}), bf16[32,48,128]{2,1,0:T(8,128)(2,1)S(1)}, u32[]{:S(2)}, u32[]{:S(2)}) %all-to-all-start) | async-done | bytes 393248 | tf_op jit(solution)/shard_map/all_to_all | solution.py:141
  61.2 8.0 %all-to-all-start.1 = ((bf16[32,48,128]{2,1,0:T(8,128)(2,1)}), bf16[32,48,128]{2,1,0:T(8,128)(2,1)S(1)}, u32[]{:S(2)}, u32[]{:S(2)}) async-start(bf16[32,48,128]{2,1,0:T(8,128)(2,1)} %fusion), calls=%async_computation.1 | async-start | bytes 786432 | tf_op jit(solution)/shard_map/all_to_all | solution.py:175
  69.2 0.0 copy-done.3
  69.2 12.3 %all-gather = bf16[1024,128]{1,0:T(8,128)(2,1)S(1)} all-gather(bf16[256,128]{1,0:T(8,128)(2,1)S(1)} %copy-done.3), channel_id=2, replica_groups=mesh['y'=8,'x'=4,'core'=2,'zl'=4,'zh'=2] {'zl'}, dimensions={0}, use_global_device_ids=true | all-gather | bytes 327680 | tf_op jit(solution)/shard_map/all_gather | solution.py:176
  81.6 1.6 %all-to-all-done.1 = bf16[32,48,128]{2,1,0:T(8,128)(2,1)S(1)} async-done(((bf16[32,48,128]{2,1,0:T(8,128)(2,1)}), bf16[32,48,128]{2,1,0:T(8,128)(2,1)S(1)}, u32[]{:S(2)}, u32[]{:S(2)}) %all-to-all-start.1) | async-done | bytes 393248 | tf_op jit(solution)/shard_map/all_to_all | solution.py:175
  83.1 0.1 convert_reduce_fusion
  83.2 0.8 broadcast_in_dim.5
  84.0 0.0 copy-start
  84.0 7.6 %all-to-all-start.2 = ((bf16[32,48,128]{2,1,0:T(8,128)(2,1)}), bf16[32,48,128]{2,1,0:T(8,128)(2,1)}, u32[]{:S(2)}, u32[]{:S(2)}) async-start(bf16[32,48,128]{2,1,0:T(8,128)(2,1)} %broadcast_in_dim.5), calls=%async_computation.2 | async-start | bytes 786432 | tf_op jit(solution)/shard_map/all_to_all | solution.py:141
  91.7 3.9 %collective-permute-start.3 = (bf16[4,256,128]{2,1,0:T(8,128)(2,1)S(1)}, bf16[4,256,128]{2,1,0:T(8,128)(2,1)S(1)}, u32[]{:S(2)}, u32[]{:S(2)}) collective-permute-start(bf16[4,256,128]{2,1,0:T(8,128)(2,1)S(1)} %bitcast.37), channel_id=1, source_target_pairs={{0,1},{1,0},{2,3},{3,2},{4,5},{5,4},{6,7},{7,6},{8,9},{9,8},{10,11... | collective-permute-start | bytes 786440 | tf_op jit(solution)/shard_map/ppermute | solution.py:132
  95.6 6.0 %all-gather.2 = bf16[64,48,128]{2,1,0:T(8,128)(2,1)S(1)} all-gather(bf16[32,48,128]{2,1,0:T(8,128)(2,1)S(1)} %all-to-all-done), channel_id=4, replica_groups=mesh['y'=8,'x'=4,'core'=2,'zl'=4,'zh'=2] {'core'}, dimensions={0}, use_global_device_ids=true | all-gather | bytes 1179648 | tf_op jit(solution)/shard_map/all_gather | solution.py:182
  101.6 1.6 %all-to-all-done.2 = bf16[32,48,128]{2,1,0:T(8,128)(2,1)} async-done(((bf16[32,48,128]{2,1,0:T(8,128)(2,1)}), bf16[32,48,128]{2,1,0:T(8,128)(2,1)}, u32[]{:S(2)}, u32[]{:S(2)}) %all-to-all-start.2) | async-done | bytes 393248 | tf_op jit(solution)/shard_map/all_to_all | solution.py:141
  103.2 7.3 %all-gather.1 = bf16[64,48,128]{2,1,0:T(8,128)(2,1)S(1)} all-gather(bf16[32,48,128]{2,1,0:T(8,128)(2,1)} %all-to-all-done.2), channel_id=3, replica_groups=mesh['y'=8,'x'=4,'core'=2,'zl'=4,'zh'=2] {'core'}, dimensions={0}, use_global_device_ids=true | all-gather | bytes 1179648 | tf_op jit(solution)/shard_map/all_gather | solution.py:183
  110.5 0.0 collective-permute-done.3.far_ref
  110.5 0.0 copy-done
  110.5 6.2 %basis_feedback_input_grad.1 = (f32[3072,128]{1,0:T(8,128)}, f32[32,128]{1,0:T(8,128)}, bf16[256,384]{1,0:T(8,128)(2,1)}) custom-call(s32[1]{0:T(128)} %bitcast.place_ref, bf16[3072,128]{1,0:T(8,128)(2,1)S(1)} %bitcast.36, f32[1536,128]{1,0:T(8,128)S(1)} %bitcast.31, f32[1536,128]{1,0:T(8,128)S(1)} %bitcast.34, f32[32,128]{1,0:T(8,128)S(1)} %bitcast.39, ...), custom_call_target="tpu_custom_call" | custom-call | flops 402653184 | bytes 5000000 | tf_op jit(solution)/shard_map/basis_feedback_input_grad/pallas_call | solution.py:107
  (3 shorter events, 0.1 us)
Async XLA Ops:
  0.6 32.7 %collective-permute-start = (bf16[48,128]{1,0:T(8,128)(2,1)}, bf16[48,128]{1,0:T(8,128)(2,1)S(1)}, u32[]{:S(2)}, u32[]{:S(2)}) collective-permute-start(bf16[48,128]{1,0:T(8,128)(2,1)} %param.7), channel_id=1, source_target_pairs={{0,0},{1,64},{2,128},{3,192},{4,256},{5,320},{6,384},{7,448},{64,1... | collective-permute-start | bytes 36872 | tf_op jit(solution)/shard_map/ppermute | solution.py:151
  2.0 31.4 %collective-permute-start.1 = (bf16[256,128]{1,0:T(8,128)(2,1)}, bf16[256,128]{1,0:T(8,128)(2,1)S(1)}, u32[]{:S(2)}, u32[]{:S(2)}) collective-permute-start(bf16[256,128]{1,0:T(8,128)(2,1)} %param.6), channel_id=1, source_target_pairs={{0,1},{1,0},{2,3},{3,2},{4,5},{5,4},{6,7},{7,6},{8,9},{9,8},{10,11... | collective-permute-start | bytes 196616 | tf_op jit(solution)/shard_map/ppermute | solution.py:132
  33.8 18.0 %copy-start.1 = (f32[3072,128]{1,0:T(8,128)S(1)}, f32[3072,128]{1,0:T(8,128)}, u32[]{:S(2)}) copy-start(f32[3072,128]{1,0:T(8,128)} %param.8) | copy-start | bytes 4718596
  33.8 17.2 %collective-permute-start.2 = (bf16[1536,128]{1,0:T(8,128)(2,1)S(1)}, bf16[1536,128]{1,0:T(8,128)(2,1)S(1)}, u32[]{:S(2)}, u32[]{:S(2)}) collective-permute-start(bf16[1536,128]{1,0:T(8,128)(2,1)S(1)} %convolution_convert_fusion), channel_id=1, source_target_pairs={{0,1},{1,0},{2,3},{3,2},{4,5},{5,4},{6,7},{7,6},{8,9},{9,8},{10,11... | collective-permute-start | bytes 1179656 | tf_op jit(solution)/shard_map/ppermute | solution.py:132
  38.1 23.1 %all-to-all-start = ((bf16[32,48,128]{2,1,0:T(8,128)(2,1)}), bf16[32,48,128]{2,1,0:T(8,128)(2,1)S(1)}, u32[]{:S(2)}, u32[]{:S(2)}) async-start(bf16[32,48,128]{2,1,0:T(8,128)(2,1)} %broadcast_in_dim.4), calls=%async_computation | async-start | bytes 786432 | tf_op jit(solution)/shard_map/all_to_all | solution.py:141
  51.0 0.7 copy-start.2
  58.9 10.3 %copy-start.3 = (bf16[256,128]{1,0:T(8,128)(2,1)S(1)}, bf16[256,128]{1,0:T(8,128)(2,1)}, u32[]{:S(2)}) copy-start(bf16[256,128]{1,0:T(8,128)(2,1)} %param.6) | copy-start | bytes 196612
  61.2 21.9 %all-to-all-start.1 = ((bf16[32,48,128]{2,1,0:T(8,128)(2,1)}), bf16[32,48,128]{2,1,0:T(8,128)(2,1)S(1)}, u32[]{:S(2)}, u32[]{:S(2)}) async-start(bf16[32,48,128]{2,1,0:T(8,128)(2,1)} %fusion), calls=%async_computation.1 | async-start | bytes 786432 | tf_op jit(solution)/shard_map/all_to_all | solution.py:175
  84.0 26.5 %copy-start = (f32[128,32]{0,1:T(8,128)S(1)}, f32[128,32]{0,1:T(8,128)}, u32[]{:S(2)}) copy-start(f32[128,32]{0,1:T(8,128)} %param.9) | copy-start | bytes 49156
  84.0 19.2 %all-to-all-start.2 = ((bf16[32,48,128]{2,1,0:T(8,128)(2,1)}), bf16[32,48,128]{2,1,0:T(8,128)(2,1)}, u32[]{:S(2)}, u32[]{:S(2)}) async-start(bf16[32,48,128]{2,1,0:T(8,128)(2,1)} %broadcast_in_dim.5), calls=%async_computation.2 | async-start | bytes 786432 | tf_op jit(solution)/shard_map/all_to_all | solution.py:141
  91.7 18.8 %collective-permute-start.3 = (bf16[4,256,128]{2,1,0:T(8,128)(2,1)S(1)}, bf16[4,256,128]{2,1,0:T(8,128)(2,1)S(1)}, u32[]{:S(2)}, u32[]{:S(2)}) collective-permute-start(bf16[4,256,128]{2,1,0:T(8,128)(2,1)S(1)} %bitcast.37), channel_id=1, source_target_pairs={{0,1},{1,0},{2,3},{3,2},{4,5},{5,4},{6,7},{7,6},{8,9},{9,8},{10,11... | collective-permute-start | bytes 786440 | tf_op jit(solution)/shard_map/ppermute | solution.py:132

commit v5 on v4

--- a/solution.py
+++ b/solution.py
@@ -22,6 +22,7 @@
 TOK = 256
 COLS = 128
 RANK = 32
+EARLY = 32
 
 
 def dot(a, b, dims, precision=None):
@@ -33,7 +34,7 @@
     fresh_ref, right_ref, input_grad_ref,
     own_buf, other_buf, fresh_buf, out_grad_buf, weight_buf, sems, out_sems,
 ):
-    zh = place_ref[0]
+    zh, zl = place_ref[0], place_ref[1]
     loads = [
         pltpu.make_async_copy(near_ref, out_grad_buf.at[0], sems.at[0]),
         pltpu.make_async_copy(far_ref, out_grad_buf.at[1], sems.at[1]),
@@ -54,9 +55,9 @@
     total = jnp.zeros((TOK, SLAB), F32)
     for half in range(2):
         side = zh if half == 0 else 1 - zh
-        for zl in range(N_ZL):
-            grads = out_grad_buf[side, zl]
-            block = (zl * 2 + half) * 4
+        for at in range(N_ZL):
+            grads = out_grad_buf[side, at]
+            block = (at * 2 + half) * 4
             rows = [weight_buf[core, block + x] for x in range(4) for core in range(2)]
             total += dot(grads, jnp.concatenate(rows, axis=0), ((1,), (1,)))
     input_grad_ref[...] = total.astype(BF)
@@ -89,7 +90,8 @@
             fresh_buf[at] = merged - approx
             half = zh if side == 0 else 1 - zh
             for slab in range(2):
-                start = pl.multiple_of(((core * 2 + slab) * 2 + half) * SLAB, SLAB)
+                owner = (zl + N_ZL - (core * 2 + slab)) % N_ZL
+                start = pl.multiple_of((owner * 2 + half) * SLAB, SLAB)
                 store = pltpu.make_async_copy(
                     fresh_buf.at[at, pl.ds(slab * SLAB, SLAB)],
                     fresh_ref.at[pl.ds(start, SLAB)],
@@ -144,18 +146,25 @@
 def on_device(features, out_grad, weight, feedback, warm_basis):
     core = lax.axis_index("core")
     zh = lax.axis_index("zh")
+    zl = lax.axis_index("zl")
     barrier = lax.optimization_barrier
 
     partner_out_grad = swap_halves(out_grad)
     plane = [(i * 8 + j, j * 8 + i) for i in range(8) for j in range(8)]
     turned = lax.ppermute(weight, ("y",) + TENSOR, plane)
 
-    gathered = lax.all_gather(features, "zl", axis=1, tiled=True)
-    gathered, turned = barrier((gathered, turned))
+    shifted = [features] + [
+        lax.ppermute(features, "zl", [(i, (i + k) % N_ZL) for i in range(N_ZL)]) for k in range(1, N_ZL)
+    ]
+    spread = jnp.broadcast_to(turned[None, :EARLY], (N_CHIP, EARLY, COLS))
+    shifted, spread = barrier((shifted, spread))
+    gathered = jnp.concatenate(shifted, axis=1)
     sent = dot(gathered, partner_out_grad, ((0,), (0,))).astype(BF)
     other_grads = swap_halves(sent)
-    chip_weights = to_all_chips(turned)
-    slabs = feedback.reshape(N_ZL, 2, SLAB, COLS)
+    early_weights = lax.all_to_all(spread, CHIPS, 0, 0)
+    natural = feedback.reshape(N_ZL, 2, SLAB, COLS)
+    slabs = [lax.dynamic_slice_in_dim(natural, (zl + N_ZL - k) % N_ZL, 1) for k in range(N_ZL)]
+    slabs = barrier(jnp.concatenate(slabs, axis=0))
 
     def add_feedback(grads, half):
         own = lax.dynamic_slice(slabs, (0, half, 0, 0), (N_ZL, 1, SLAB, COLS))
@@ -171,17 +180,21 @@
     swapped = lax.all_gather(quarters(1 - core).astype(BF), "core", axis=0)
     chips = (quarters(core) + pick(swapped, 1 - core).astype(F32)).astype(BF).reshape(N_CHIP, PIECE, COLS)
 
-    chips, chip_weights, late = barrier((chips, chip_weights, out_grad))
-    parts = lax.all_to_all(chips, CHIPS, 0, 0)
+    late_weight = jnp.broadcast_to(turned[None, EARLY:], (N_CHIP, PIECE - EARLY, COLS))
+    load = jnp.concatenate([chips, late_weight], axis=1)
+    load, early_weights, late = barrier((load, early_weights, out_grad))
+    arrived = lax.all_to_all(load, CHIPS, 0, 0)
     near = lax.all_gather(late, "zl", axis=0)
-    parts, near = barrier((parts, near))
+    arrived, near = barrier((arrived, near))
+    parts = arrived[:, :PIECE]
 
     piece = (jnp.sum(parts.astype(F32), axis=0) / REPLICAS).astype(BF)
-    piece, chip_weights, near = barrier((piece, chip_weights, near))
+    piece, early_weights, arrived, near = barrier((piece, early_weights, arrived, near))
+    chip_weights = jnp.concatenate([early_weights, arrived[:, PIECE:]], axis=1)
     far = swap_halves(near)
     weights = lax.all_gather(chip_weights, "core", axis=0)
     all_means = lax.all_gather(to_all_chips(piece), "core", axis=0).reshape(D_IN, COLS)
-    place = zh.astype(jnp.int32).reshape(1)
+    place = jnp.stack([zh, zl]).astype(jnp.int32)
     new_feedback, right, input_grad = tail_call(
         place, all_means, own_merged, other_merged, warm_basis.T, near, far, weights
     )

time: 117 us -> 115 us (0.983)
  blocking collectives: 56.9 us -> 31.3 us
  starting transfers between devices: 41.8 us -> 55 us
  waiting for transfers between devices: 4.72 us -> 9.74 us
  local copies, waits for them, and re-layouts: 2.5 us -> 4.67 us
  other arithmetic: 2.18 us -> 3.46 us
    all_gather x1 -> x0, blocking collectives: 25.6 us -> none  [on_device(): gathered = lax.all_gather(features, 'zl', axis=1, tiled=True)]
    ppermute x0 -> x3, starting transfers between devices: none -> 18.9 us  [on_device(): lax.ppermute(features, 'zl', [(i, (i + k) % N_ZL) for i in range(N_ZL)])]
    all_to_all x2 -> x1, starting transfers between devices: 19.2 us -> 5.17 us  [to_all_chips(): return lax.all_to_all(spread, CHIPS, 0, 0)]
    all_to_all x1 -> x2, starting transfers between devices: 7.97 us -> 18.5 us  [the longest x1 10 us: on_device(): early_weights = lax.all_to_all(spread, CHIPS, 0, 0)]
    all_to_all x1 -> x2, waiting for transfers between devices: 1.56 us -> 4.87 us  [the longest x1 3.94 us: on_device(): arrived = lax.all_to_all(load, CHIPS, 0, 0)]
    ppermute x0 -> x3, waiting for transfers between devices: none -> 3.03 us  [on_device(): lax.ppermute(features, 'zl', [(i, (i + k) % N_ZL) for i in range(N_ZL)])]
    ppermute x3, starting transfers between devices: 13.2 us -> 11.1 us  [swap_halves(): return lax.ppermute(block, 'zh', [(0, 1), (1, 0)])]
    all_to_all x2 -> x1, waiting for transfers between devices: 3.15 us -> 1.08 us  [to_all_chips(): return lax.all_to_all(spread, CHIPS, 0, 0)]
  transfers between devices with their start and end apart: 7 -> 10, of which waited for: 3 -> 5; matrix products, arithmetic and copies ran while one was open for 4% -> 7% of each run, Pallas kernels for 0% -> 0%
where the time goes in v5:
time: 115 us; the launch traced here: 114 us
  starting transfers between devices  55 us (48%)
  blocking collectives  31.3 us (27%)
  waiting for transfers between devices  9.74 us (8%)
  Pallas kernels  6.75 us (6%)
  local copies, waits for them, and re-layouts  4.67 us (4%)
  other arithmetic  3.46 us (3%)
  matrix products  2.42 us (2%)
    ppermute x3, starting transfers between devices, on_device(): lax.ppermute(features, 'zl', [(i, (i + k) % N_ZL) for i in range(N_ZL)])  18.9 us
    all_gather x1, blocking collectives, on_device(): near = lax.all_gather(late, 'zl', axis=0)  12.6 us
    ppermute x3, starting transfers between devices, swap_halves(): return lax.ppermute(block, 'zh', [(0, 1), (1, 0)])  11.1 us
    all_to_all x1, starting transfers between devices, on_device(): early_weights = lax.all_to_all(spread, CHIPS, 0, 0)  10 us
    all_to_all x1, starting transfers between devices, on_device(): arrived = lax.all_to_all(load, CHIPS, 0, 0)  8.49 us
    all_gather x1, blocking collectives, on_device(): lax.all_gather(to_all_chips(piece), 'core', axis=0).reshape(D_IN, COLS)  7.28 us
    pallas_call x1, Pallas kernels, tail_call(): pl.pallas_call(tail_kernel, in_specs=[pl.BlockSpec(memory_space=pltpu.SME...  6.75 us
    all_gather x1, blocking collectives, on_device(): weights = lax.all_gather(chip_weights, 'core', axis=0)  6.17 us
  transfers between devices with their start and end apart: 10, of which 5 were waited for; matrix products, arithmetic and copies ran while one was open for 7% of the time, Pallas kernels for 0%

profile of v5, /device:TPU:1, one launch (start us, length us, event | category | flops | bytes accessed | tf_op | source)
XLA Modules:
  0.0 114.3 jit_solution(5492449742740839094)
XLA Ops:
  0.6 11.5 %collective-permute-start.1 = (bf16[256,384]{1,0:T(8,128)(2,1)}, bf16[256,384]{1,0:T(8,128)(2,1)S(1)}, u32[]{:S(2)}, u32[]{:S(2)}) collective-permute-start(bf16[256,384]{1,0:T(8,128)(2,1)} %param.5), channel_id=1, source_target_pairs={{0,4},{2,6},{4,0},{6,2},{1,5},{3,7},{5,1},{7,3},{8,12},{10,14},{12... | collective-permute-start | bytes 589832 | tf_op jit(solution)/shard_map/ppermute | solution.py:157
  12.1 4.0 %collective-permute-start = (bf16[256,384]{1,0:T(8,128)(2,1)}, bf16[256,384]{1,0:T(8,128)(2,1)S(1)}, u32[]{:S(2)}, u32[]{:S(2)}) collective-permute-start(bf16[256,384]{1,0:T(8,128)(2,1)} %param.5), channel_id=1, source_target_pairs={{0,2},{2,4},{4,6},{6,0},{1,3},{3,5},{5,7},{7,1},{8,10},{10,12},{12... | collective-permute-start | bytes 589832 | tf_op jit(solution)/shard_map/ppermute | solution.py:157
  16.1 3.4 %collective-permute-start.2 = (bf16[256,384]{1,0:T(8,128)(2,1)}, bf16[256,384]{1,0:T(8,128)(2,1)S(1)}, u32[]{:S(2)}, u32[]{:S(2)}) collective-permute-start(bf16[256,384]{1,0:T(8,128)(2,1)} %param.5), channel_id=1, source_target_pairs={{0,6},{2,0},{4,2},{6,4},{1,7},{3,1},{5,3},{7,5},{8,14},{10,8},{12,... | collective-permute-start | bytes 589832 | tf_op jit(solution)/shard_map/ppermute | solution.py:157
  19.5 1.4 %collective-permute-start.3 = (bf16[48,128]{1,0:T(8,128)(2,1)}, bf16[48,128]{1,0:T(8,128)(2,1)S(1)}, u32[]{:S(2)}, u32[]{:S(2)}) collective-permute-start(bf16[48,128]{1,0:T(8,128)(2,1)} %param.7), channel_id=1, source_target_pairs={{0,0},{1,64},{2,128},{3,192},{4,256},{5,320},{6,384},{7,448},{64,1... | collective-permute-start | bytes 36872 | tf_op jit(solution)/shard_map/ppermute | solution.py:154
  20.9 4.9 %collective-permute-start.4 = (bf16[256,128]{1,0:T(8,128)(2,1)}, bf16[256,128]{1,0:T(8,128)(2,1)S(1)}, u32[]{:S(2)}, u32[]{:S(2)}) collective-permute-start(bf16[256,128]{1,0:T(8,128)(2,1)} %param.6), channel_id=1, source_target_pairs={{0,1},{1,0},{2,3},{3,2},{4,5},{5,4},{6,7},{7,6},{8,9},{9,8},{10,11... | collective-permute-start | bytes 196616 | tf_op jit(solution)/shard_map/ppermute | solution.py:134
  25.9 0.0 copy-start.3
  25.9 2.3 %dynamic-slice_bitcast_fusion.3 = (f32[1,2,384,128]{3,2,0,1:T(8,128)S(1)}, f32[1,2,384,128]{3,2,0,1:T(8,128)S(1)}, f32[1,2,384,128]{3,2,0,1:T(8,128)S(1)}, f32[1,2,384,128]{3,2,0,1:T(8,128)}) fusion(f32[4,2,384,128]{3,2,1,0:T(8,128)} %bitcast.47, s32[]{:T(128)S(6)} %select_n.49, s32[]{:T(128)S(6)} %select_n.53, s32[]{:T(128)S(6)} %select_n.51, s32[]{:T(128)S(6)} %select_n.55), kind=kLoop, calls=%fused_computation.16 | loop fusion | bytes 3145744
  28.1 0.0 copy-start.1
  28.2 0.0 collective-permute-done.3
  28.2 0.0 copy-start.4
  28.2 0.0 collective-permute-done.1
  28.2 0.0 collective-permute-done
  28.2 3.0 %collective-permute-done.2 = bf16[256,384]{1,0:T(8,128)(2,1)S(1)} collective-permute-done((bf16[256,384]{1,0:T(8,128)(2,1)}, bf16[256,384]{1,0:T(8,128)(2,1)S(1)}, u32[]{:S(2)}, u32[]{:S(2)}) %collective-permute-start.2) | collective-permute-done | bytes 196640 | tf_op jit(solution)/shard_map/ppermute | solution.py:157
  31.2 0.7 broadcast_in_dim.6
  32.0 0.0 copy-done.3
  32.1 0.7 collective-permute-done.4
  32.9 1.2 %convolution_convert_fusion = bf16[1536,128]{1,0:T(8,128)(2,1)} fusion(bf16[256,1536]{1,0:T(8,128)(2,1)S(1)} %constant_dynamic-update-slice_fusion, bf16[256,128]{1,0:T(8,128)(2,1)S(1)} %collective-permute-done.4), kind=kOutput, calls=%fused_computation | convolution fusion | flops 100859904 | bytes 1245184 | tf_op jit(solution)/shard_map/dot_general | solution.py:29
  34.0 3.1 %collective-permute-start.5 = (bf16[1536,128]{1,0:T(8,128)(2,1)}, bf16[1536,128]{1,0:T(8,128)(2,1)}, u32[]{:S(2)}, u32[]{:S(2)}) collective-permute-start(bf16[1536,128]{1,0:T(8,128)(2,1)} %convolution_convert_fusion), channel_id=1, source_target_pairs={{0,1},{1,0},{2,3},{3,2},{4,5},{5,4},{6,7},{7,6},{8,9},{9,8},{10,11... | collective-permute-start | bytes 1179656 | tf_op jit(solution)/shard_map/ppermute | solution.py:134
  37.1 0.0 copy-done.1
  37.1 0.1 pad_maximum_fusion
  37.2 0.0 copy-done.4
  37.2 10.0 %all-to-all-start = ((bf16[32,32,128]{2,1,0:T(8,128)(2,1)}), bf16[32,32,128]{2,1,0:T(8,128)(2,1)}, u32[]{:S(2)}, u32[]{:S(2)}) async-start(bf16[32,32,128]{2,1,0:T(8,128)(2,1)} %broadcast_in_dim.6), calls=%async_computation | async-start | bytes 524288 | tf_op jit(solution)/shard_map/all_to_all | solution.py:164
  47.3 1.2 %fusion.3 = f32[1536,128]{1,0:T(8,128)S(1)} fusion(bf16[256,1536]{1,0:T(8,128)(2,1)S(1)} %constant_dynamic-update-slice_fusion, bf16[256,128]{1,0:T(8,128)(2,1)} %param.6), kind=kOutput, calls=%fused_computation.28 | convolution fusion | flops 100663296 | bytes 1638400 | tf_op jit(solution)/shard_map/dot_general | solution.py:29
  48.5 0.0 collective-permute-done.5
  48.5 1.2 %dynamic-slice_add_fusion = (f32[4,1,384,128]{3,2,0,1:T(8,128)S(1)}, f32[4,1,384,128]{3,2,0,1:T(8,128)S(1)}) fusion(f32[4,1,384,128]{3,2,0,1:T(8,128)S(1)} %bitcast.45, f32[4,2,384,128]{3,2,0,1:T(8,128)S(1)} %pad_maximum_fusion, s32[]{:T(128)S(6)} %select_n.56, s32[]{:T(128)S(6)} %select_n.58, bf16[4,1,384,128]{3,2,0,1:T(8,128)(2,1)} %bitcast.18), kind=kLoop, calls=%fused_computation.7 | loop fusion | flops 589824 | bytes 4325384 | tf_op jit(solution)/shard_map/add | solution.py:171
  49.7 0.1 fusion.1
  49.9 5.2 %all_gather.22 = bf16[2,2,768,128]{3,2,1,0:T(8,128)(2,1)S(1)} all-gather(bf16[1,2,768,128]{3,2,1,0:T(8,128)(2,1)S(1)} %pad_maximum_fusion.3), channel_id=1, replica_groups=mesh['y'=8,'x'=4,'core'=2,'zl'=4,'zh'=2] {'core'}, dimensions={0}, use_global_device_ids=true | all-gather | bytes 1179648 | tf_op jit(solution)/shard_map/all_gather | solution.py:180
  55.0 0.1 constant_dynamic-slice_fusion.1
  55.1 0.1 pad_maximum_fusion.1
  55.2 0.0 slice-start
  55.2 0.0 copy-start.2
  55.2 0.1 fusion
  55.3 0.5 slice-done
  55.9 0.9 pad_maximum_fusion.2
  56.7 0.9 all-to-all-done
  57.7 8.5 %all-to-all-start.1 = ((bf16[32,64,128]{2,1,0:T(8,128)(2,1)}), bf16[32,64,128]{2,1,0:T(8,128)(2,1)S(1)}, u32[]{:S(2)}, u32[]{:S(2)}) async-start(bf16[32,64,128]{2,1,0:T(8,128)(2,1)} %pad_maximum_fusion.2), calls=%async_computation.1 | async-start | bytes 1048576 | tf_op jit(solution)/shard_map/all_to_all | solution.py:186
  66.2 0.0 copy-done.2
  66.2 12.6 %all-gather = bf16[1024,128]{1,0:T(8,128)(2,1)S(1)} all-gather(bf16[256,128]{1,0:T(8,128)(2,1)S(1)} %copy-done.2), channel_id=2, replica_groups=mesh['y'=8,'x'=4,'core'=2,'zl'=4,'zh'=2] {'zl'}, dimensions={0}, use_global_device_ids=true | all-gather | bytes 327680 | tf_op jit(solution)/shard_map/all_gather | solution.py:187
  78.8 3.9 %all-to-all-done.1 = bf16[32,64,128]{2,1,0:T(8,128)(2,1)S(1)} async-done(((bf16[32,64,128]{2,1,0:T(8,128)(2,1)}), bf16[32,64,128]{2,1,0:T(8,128)(2,1)S(1)}, u32[]{:S(2)}, u32[]{:S(2)}) %all-to-all-start.1) | async-done | bytes 524320 | tf_op jit(solution)/shard_map/all_to_all | solution.py:186
  82.7 0.1 convert_reduce_fusion
  82.8 0.8 broadcast_in_dim.8
  83.6 5.2 %all-to-all-start.2 = ((bf16[32,48,128]{2,1,0:T(8,128)(2,1)}), bf16[32,48,128]{2,1,0:T(8,128)(2,1)S(1)}, u32[]{:S(2)}, u32[]{:S(2)}) async-start(bf16[32,48,128]{2,1,0:T(8,128)(2,1)} %broadcast_in_dim.8), calls=%async_computation.2 | async-start | bytes 786432 | tf_op jit(solution)/shard_map/all_to_all | solution.py:143
  88.8 0.1 pad_add_fusion.place_ref
  88.9 0.0 copy-start
  88.9 3.1 %collective-permute-start.6 = (bf16[4,256,128]{2,1,0:T(8,128)(2,1)S(1)}, bf16[4,256,128]{2,1,0:T(8,128)(2,1)S(1)}, u32[]{:S(2)}, u32[]{:S(2)}) collective-permute-start(bf16[4,256,128]{2,1,0:T(8,128)(2,1)S(1)} %bitcast.42), channel_id=1, source_target_pairs={{0,1},{1,0},{2,3},{3,2},{4,5},{5,4},{6,7},{7,6},{8,9},{9,8},{10,11... | collective-permute-start | bytes 786440 | tf_op jit(solution)/shard_map/ppermute | solution.py:134
  92.0 1.0 pad_maximum_fusion.4
  93.0 6.2 %all-gather.2 = bf16[64,48,128]{2,1,0:T(8,128)(2,1)S(1)} all-gather(bf16[32,48,128]{2,1,0:T(8,128)(2,1)S(1)} %pad_maximum_fusion.4), channel_id=4, replica_groups=mesh['y'=8,'x'=4,'core'=2,'zl'=4,'zh'=2] {'core'}, dimensions={0}, use_global_device_ids=true | all-gather | bytes 1179648 | tf_op jit(solution)/shard_map/all_gather | solution.py:195
  99.2 1.1 all-to-all-done.2
  100.3 7.3 %all-gather.1 = bf16[64,48,128]{2,1,0:T(8,128)(2,1)S(1)} all-gather(bf16[32,48,128]{2,1,0:T(8,128)(2,1)S(1)} %all-to-all-done.2), channel_id=3, replica_groups=mesh['y'=8,'x'=4,'core'=2,'zl'=4,'zh'=2] {'core'}, dimensions={0}, use_global_device_ids=true | all-gather | bytes 1179648 | tf_op jit(solution)/shard_map/all_gather | solution.py:196
  107.5 0.0 collective-permute-done.6.far_ref
  107.5 0.0 copy-done
  107.5 6.8 %basis_feedback_input_grad.1 = (f32[3072,128]{1,0:T(8,128)}, f32[32,128]{1,0:T(8,128)}, bf16[256,384]{1,0:T(8,128)(2,1)}) custom-call(s32[2]{0:T(128)S(1)} %pad_add_fusion.place_ref, bf16[3072,128]{1,0:T(8,128)(2,1)S(1)} %bitcast.41, f32[1536,128]{1,0:T(8,128)S(1)} %bitcast.36, f32[1536,128]{1,0:T(8,128)S(1)} %bitcast.39, f32[32,128]{1,0:T(8,128)S(1)} %bitcast.44, ...), custom_call_target="tpu_custom_call" | custom-call | flops 402653184 | bytes 5000000 | tf_op jit(solution)/shard_map/basis_feedback_input_grad/pallas_call | solution.py:109
  (10 shorter events, 0.2 us)
Async XLA Ops:
  0.6 27.5 %collective-permute-start.1 = (bf16[256,384]{1,0:T(8,128)(2,1)}, bf16[256,384]{1,0:T(8,128)(2,1)S(1)}, u32[]{:S(2)}, u32[]{:S(2)}) collective-permute-start(bf16[256,384]{1,0:T(8,128)(2,1)} %param.5), channel_id=1, source_target_pairs={{0,4},{2,6},{4,0},{6,2},{1,5},{3,7},{5,1},{7,3},{8,12},{10,14},{12... | collective-permute-start | bytes 589832 | tf_op jit(solution)/shard_map/ppermute | solution.py:157
  12.1 16.1 %collective-permute-start = (bf16[256,384]{1,0:T(8,128)(2,1)}, bf16[256,384]{1,0:T(8,128)(2,1)S(1)}, u32[]{:S(2)}, u32[]{:S(2)}) collective-permute-start(bf16[256,384]{1,0:T(8,128)(2,1)} %param.5), channel_id=1, source_target_pairs={{0,2},{2,4},{4,6},{6,0},{1,3},{3,5},{5,7},{7,1},{8,10},{10,12},{12... | collective-permute-start | bytes 589832 | tf_op jit(solution)/shard_map/ppermute | solution.py:157
  16.1 15.1 %collective-permute-start.2 = (bf16[256,384]{1,0:T(8,128)(2,1)}, bf16[256,384]{1,0:T(8,128)(2,1)S(1)}, u32[]{:S(2)}, u32[]{:S(2)}) collective-permute-start(bf16[256,384]{1,0:T(8,128)(2,1)} %param.5), channel_id=1, source_target_pairs={{0,6},{2,0},{4,2},{6,4},{1,7},{3,1},{5,3},{7,5},{8,14},{10,8},{12,... | collective-permute-start | bytes 589832 | tf_op jit(solution)/shard_map/ppermute | solution.py:157
  19.5 8.6 %collective-permute-start.3 = (bf16[48,128]{1,0:T(8,128)(2,1)}, bf16[48,128]{1,0:T(8,128)(2,1)S(1)}, u32[]{:S(2)}, u32[]{:S(2)}) collective-permute-start(bf16[48,128]{1,0:T(8,128)(2,1)} %param.7), channel_id=1, source_target_pairs={{0,0},{1,64},{2,128},{3,192},{4,256},{5,320},{6,384},{7,448},{64,1... | collective-permute-start | bytes 36872 | tf_op jit(solution)/shard_map/ppermute | solution.py:154
  20.9 12.0 %collective-permute-start.4 = (bf16[256,128]{1,0:T(8,128)(2,1)}, bf16[256,128]{1,0:T(8,128)(2,1)S(1)}, u32[]{:S(2)}, u32[]{:S(2)}) collective-permute-start(bf16[256,128]{1,0:T(8,128)(2,1)} %param.6), channel_id=1, source_target_pairs={{0,1},{1,0},{2,3},{3,2},{4,5},{5,4},{6,7},{7,6},{8,9},{9,8},{10,11... | collective-permute-start | bytes 196616 | tf_op jit(solution)/shard_map/ppermute | solution.py:134
  25.9 6.1 %copy-start.3 = (bf16[256,384]{1,0:T(8,128)(2,1)S(1)}, bf16[256,384]{1,0:T(8,128)(2,1)}, u32[]{:S(2)}) copy-start(bf16[256,384]{1,0:T(8,128)(2,1)} %param.5) | copy-start | bytes 589828
  28.1 9.0 %copy-start.1 = (f32[1,2,384,128]{3,2,0,1:T(8,128)S(1)}, f32[1,2,384,128]{3,2,0,1:T(8,128)}, u32[]{:S(2)}) copy-start(f32[1,2,384,128]{3,2,0,1:T(8,128)} %get-tuple-element.42) | copy-start | bytes 1179652
  28.2 9.1 %copy-start.4 = (bf16[48,128]{1,0:T(8,128)(2,1)}, bf16[48,128]{1,0:T(8,128)(2,1)S(1)}, u32[]{:S(2)}) copy-start(bf16[48,128]{1,0:T(8,128)(2,1)S(1)} %collective-permute-done.3) | copy-start | bytes 36868
  34.0 14.5 %collective-permute-start.5 = (bf16[1536,128]{1,0:T(8,128)(2,1)}, bf16[1536,128]{1,0:T(8,128)(2,1)}, u32[]{:S(2)}, u32[]{:S(2)}) collective-permute-start(bf16[1536,128]{1,0:T(8,128)(2,1)} %convolution_convert_fusion), channel_id=1, source_target_pairs={{0,1},{1,0},{2,3},{3,2},{4,5},{5,4},{6,7},{7,6},{8,9},{9,8},{10,11... | collective-permute-start | bytes 1179656 | tf_op jit(solution)/shard_map/ppermute | solution.py:134
  37.2 20.4 %all-to-all-start = ((bf16[32,32,128]{2,1,0:T(8,128)(2,1)}), bf16[32,32,128]{2,1,0:T(8,128)(2,1)}, u32[]{:S(2)}, u32[]{:S(2)}) async-start(bf16[32,32,128]{2,1,0:T(8,128)(2,1)} %broadcast_in_dim.6), calls=%async_computation | async-start | bytes 524288 | tf_op jit(solution)/shard_map/all_to_all | solution.py:164
  55.2 0.7 slice-start
  55.2 10.9 %copy-start.2 = (bf16[256,128]{1,0:T(8,128)(2,1)S(1)}, bf16[256,128]{1,0:T(8,128)(2,1)}, u32[]{:S(2)}) copy-start(bf16[256,128]{1,0:T(8,128)(2,1)} %param.6) | copy-start | bytes 196612
  57.7 25.1 %all-to-all-start.1 = ((bf16[32,64,128]{2,1,0:T(8,128)(2,1)}), bf16[32,64,128]{2,1,0:T(8,128)(2,1)S(1)}, u32[]{:S(2)}, u32[]{:S(2)}) async-start(bf16[32,64,128]{2,1,0:T(8,128)(2,1)} %pad_maximum_fusion.2), calls=%async_computation.1 | async-start | bytes 1048576 | tf_op jit(solution)/shard_map/all_to_all | solution.py:186
  83.6 16.6 %all-to-all-start.2 = ((bf16[32,48,128]{2,1,0:T(8,128)(2,1)}), bf16[32,48,128]{2,1,0:T(8,128)(2,1)S(1)}, u32[]{:S(2)}, u32[]{:S(2)}) async-start(bf16[32,48,128]{2,1,0:T(8,128)(2,1)} %broadcast_in_dim.8), calls=%async_computation.2 | async-start | bytes 786432 | tf_op jit(solution)/shard_map/all_to_all | solution.py:143
  88.9 18.6 %copy-start = (f32[128,32]{0,1:T(8,128)S(1)}, f32[128,32]{0,1:T(8,128)}, u32[]{:S(2)}) copy-start(f32[128,32]{0,1:T(8,128)} %param.9) | copy-start | bytes 49156
  88.9 18.6 %collective-permute-start.6 = (bf16[4,256,128]{2,1,0:T(8,128)(2,1)S(1)}, bf16[4,256,128]{2,1,0:T(8,128)(2,1)S(1)}, u32[]{:S(2)}, u32[]{:S(2)}) collective-permute-start(bf16[4,256,128]{2,1,0:T(8,128)(2,1)S(1)} %bitcast.42), channel_id=1, source_target_pairs={{0,1},{1,0},{2,3},{3,2},{4,5},{5,4},{6,7},{7,6},{8,9},{9,8},{10,11... | collective-permute-start | bytes 786440 | tf_op jit(solution)/shard_map/ppermute | solution.py:134

commit v6 on v5

--- a/solution.py
+++ b/solution.py
@@ -182,21 +182,22 @@
 
     late_weight = jnp.broadcast_to(turned[None, EARLY:], (N_CHIP, PIECE - EARLY, COLS))
     load = jnp.concatenate([chips, late_weight], axis=1)
-    load, early_weights, late = barrier((load, early_weights, out_grad))
+    load, early_weights, late, late_grads = barrier((load, early_weights, out_grad, other_grads))
     arrived = lax.all_to_all(load, CHIPS, 0, 0)
     near = lax.all_gather(late, "zl", axis=0)
-    arrived, near = barrier((arrived, near))
+    arrived, near, late_grads = barrier((arrived, near, late_grads))
     parts = arrived[:, :PIECE]
 
     piece = (jnp.sum(parts.astype(F32), axis=0) / REPLICAS).astype(BF)
-    piece, early_weights, arrived, near = barrier((piece, early_weights, arrived, near))
+    piece, early_weights, arrived, near, late_grads = barrier((piece, early_weights, arrived, near, late_grads))
     chip_weights = jnp.concatenate([early_weights, arrived[:, PIECE:]], axis=1)
     far = swap_halves(near)
+    late_merged = add_feedback(late_grads, 1 - zh)
     weights = lax.all_gather(chip_weights, "core", axis=0)
     all_means = lax.all_gather(to_all_chips(piece), "core", axis=0).reshape(D_IN, COLS)
     place = jnp.stack([zh, zl]).astype(jnp.int32)
     new_feedback, right, input_grad = tail_call(
-        place, all_means, own_merged, other_merged, warm_basis.T, near, far, weights
+        place, all_means, own_merged, late_merged, warm_basis.T, near, far, weights
     )
     return (input_grad, new_feedback, right.T)
 

time: 115 us -> 114 us (level)
    unnamed x14 -> x20, local copies, waits for them, and re-layouts: 2.37 us -> 2.51 us
  transfers between devices with their start and end apart: 10 -> 10, of which waited for: 5 -> 4; matrix products, arithmetic and copies ran while one was open for 7% -> 7% of each run, Pallas kernels for 0% -> 0%
where the time goes in v6:
time: 114 us; the launch traced here: 113 us
  starting transfers between devices  54.2 us (48%)
  blocking collectives  30.6 us (27%)
  waiting for transfers between devices  9.58 us (8%)
  Pallas kernels  6.75 us (6%)
  local copies, waits for them, and re-layouts  4.86 us (4%)
  other arithmetic  3.68 us (3%)
  matrix products  2.41 us (2%)
    ppermute x3, starting transfers between devices, on_device(): lax.ppermute(features, 'zl', [(i, (i + k) % N_ZL) for i in range(N_ZL)])  18.9 us
    all_gather x1, blocking collectives, on_device(): near = lax.all_gather(late, 'zl', axis=0)  12.3 us
    ppermute x3, starting transfers between devices, swap_halves(): return lax.ppermute(block, 'zh', [(0, 1), (1, 0)])  11.3 us
    all_to_all x1, starting transfers between devices, on_device(): early_weights = lax.all_to_all(spread, CHIPS, 0, 0)  9.9 us
    all_to_all x1, starting transfers between devices, on_device(): arrived = lax.all_to_all(load, CHIPS, 0, 0)  7.61 us
    all_gather x1, blocking collectives, on_device(): lax.all_gather(to_all_chips(piece), 'core', axis=0).reshape(D_IN, COLS)  7.03 us
    pallas_call x1, Pallas kernels, tail_call(): pl.pallas_call(tail_kernel, in_specs=[pl.BlockSpec(memory_space=pltpu.SME...  6.75 us
    all_gather x1, blocking collectives, on_device(): weights = lax.all_gather(chip_weights, 'core', axis=0)  6.1 us
  transfers between devices with their start and end apart: 10, of which 4 were waited for; matrix products, arithmetic and copies ran while one was open for 7% of the time, Pallas kernels for 0%

profile of v6, /device:TPU:1, one launch (start us, length us, event | category | flops | bytes accessed | tf_op | source)
XLA Modules:
  0.0 113.1 jit_solution(6148762262678076221)
XLA Ops:
  0.6 11.5 %collective-permute-start.1 = (bf16[256,384]{1,0:T(8,128)(2,1)}, bf16[256,384]{1,0:T(8,128)(2,1)S(1)}, u32[]{:S(2)}, u32[]{:S(2)}) collective-permute-start(bf16[256,384]{1,0:T(8,128)(2,1)} %param.5), channel_id=1, source_target_pairs={{0,4},{2,6},{4,0},{6,2},{1,5},{3,7},{5,1},{7,3},{8,12},{10,14},{12... | collective-permute-start | bytes 589832 | tf_op jit(solution)/shard_map/ppermute | solution.py:157
  12.1 4.0 %collective-permute-start = (bf16[256,384]{1,0:T(8,128)(2,1)}, bf16[256,384]{1,0:T(8,128)(2,1)S(1)}, u32[]{:S(2)}, u32[]{:S(2)}) collective-permute-start(bf16[256,384]{1,0:T(8,128)(2,1)} %param.5), channel_id=1, source_target_pairs={{0,2},{2,4},{4,6},{6,0},{1,3},{3,5},{5,7},{7,1},{8,10},{10,12},{12... | collective-permute-start | bytes 589832 | tf_op jit(solution)/shard_map/ppermute | solution.py:157
  16.1 3.4 %collective-permute-start.2 = (bf16[256,384]{1,0:T(8,128)(2,1)}, bf16[256,384]{1,0:T(8,128)(2,1)S(1)}, u32[]{:S(2)}, u32[]{:S(2)}) collective-permute-start(bf16[256,384]{1,0:T(8,128)(2,1)} %param.5), channel_id=1, source_target_pairs={{0,6},{2,0},{4,2},{6,4},{1,7},{3,1},{5,3},{7,5},{8,14},{10,8},{12,... | collective-permute-start | bytes 589832 | tf_op jit(solution)/shard_map/ppermute | solution.py:157
  19.5 1.4 %collective-permute-start.3 = (bf16[48,128]{1,0:T(8,128)(2,1)}, bf16[48,128]{1,0:T(8,128)(2,1)S(1)}, u32[]{:S(2)}, u32[]{:S(2)}) collective-permute-start(bf16[48,128]{1,0:T(8,128)(2,1)} %param.7), channel_id=1, source_target_pairs={{0,0},{1,64},{2,128},{3,192},{4,256},{5,320},{6,384},{7,448},{64,1... | collective-permute-start | bytes 36872 | tf_op jit(solution)/shard_map/ppermute | solution.py:154
  20.9 4.9 %collective-permute-start.4 = (bf16[256,128]{1,0:T(8,128)(2,1)}, bf16[256,128]{1,0:T(8,128)(2,1)S(1)}, u32[]{:S(2)}, u32[]{:S(2)}) collective-permute-start(bf16[256,128]{1,0:T(8,128)(2,1)} %param.6), channel_id=1, source_target_pairs={{0,1},{1,0},{2,3},{3,2},{4,5},{5,4},{6,7},{7,6},{8,9},{9,8},{10,11... | collective-permute-start | bytes 196616 | tf_op jit(solution)/shard_map/ppermute | solution.py:134
  25.9 0.0 copy-start.6
  25.9 2.4 %dynamic-slice_bitcast_fusion.3 = (f32[1,2,384,128]{3,2,0,1:T(8,128)S(1)}, f32[1,2,384,128]{3,2,0,1:T(8,128)S(1)}, f32[1,2,384,128]{3,2,0,1:T(8,128)}, f32[1,2,384,128]{3,2,0,1:T(8,128)}) fusion(f32[4,2,384,128]{3,2,1,0:T(8,128)} %bitcast.51, s32[]{:T(128)S(6)} %select_n.50, s32[]{:T(128)S(6)} %select_n.54, s32[]{:T(128)S(6)} %select_n.52, s32[]{:T(128)S(6)} %select_n.56), kind=kLoop, calls=%fused_computation.17 | loop fusion | bytes 3145744
  28.3 0.0 copy-start.2
  28.3 0.0 copy-start.3
  28.3 0.0 collective-permute-done.3
  28.3 0.0 copy-start.7
  28.3 0.0 collective-permute-done.1
  28.3 0.0 collective-permute-done
  28.3 2.9 %collective-permute-done.2 = bf16[256,384]{1,0:T(8,128)(2,1)S(1)} collective-permute-done((bf16[256,384]{1,0:T(8,128)(2,1)}, bf16[256,384]{1,0:T(8,128)(2,1)S(1)}, u32[]{:S(2)}, u32[]{:S(2)}) %collective-permute-start.2) | collective-permute-done | bytes 196640 | tf_op jit(solution)/shard_map/ppermute | solution.py:157
  31.2 0.7 broadcast_in_dim.6
  32.0 0.0 copy-done.6
  32.1 0.7 collective-permute-done.4
  32.9 1.2 %convolution_convert_fusion = bf16[1536,128]{1,0:T(8,128)(2,1)} fusion(bf16[256,1536]{1,0:T(8,128)(2,1)S(1)} %constant_dynamic-update-slice_fusion, bf16[256,128]{1,0:T(8,128)(2,1)S(1)} %collective-permute-done.4), kind=kOutput, calls=%fused_computation | convolution fusion | flops 100859904 | bytes 1245184 | tf_op jit(solution)/shard_map/dot_general | solution.py:29
  34.0 3.1 %collective-permute-start.5 = (bf16[1536,128]{1,0:T(8,128)(2,1)}, bf16[1536,128]{1,0:T(8,128)(2,1)S(1)}, u32[]{:S(2)}, u32[]{:S(2)}) collective-permute-start(bf16[1536,128]{1,0:T(8,128)(2,1)} %convolution_convert_fusion), channel_id=1, source_target_pairs={{0,1},{1,0},{2,3},{3,2},{4,5},{5,4},{6,7},{7,6},{8,9},{9,8},{10,11... | collective-permute-start | bytes 1179656 | tf_op jit(solution)/shard_map/ppermute | solution.py:134
  37.1 0.0 copy-done.2
  37.1 0.0 copy-done.3
  37.1 0.1 pad_maximum_fusion
  37.2 0.0 copy-start.1
  37.2 0.0 copy-done.7
  37.2 9.9 %all-to-all-start = ((bf16[32,32,128]{2,1,0:T(8,128)(2,1)}), bf16[32,32,128]{2,1,0:T(8,128)(2,1)S(1)}, u32[]{:S(2)}, u32[]{:S(2)}) async-start(bf16[32,32,128]{2,1,0:T(8,128)(2,1)} %broadcast_in_dim.6), calls=%async_computation | async-start | bytes 524288 | tf_op jit(solution)/shard_map/all_to_all | solution.py:164
  47.2 1.2 %fusion.3 = f32[1536,128]{1,0:T(8,128)S(1)} fusion(bf16[256,1536]{1,0:T(8,128)(2,1)S(1)} %constant_dynamic-update-slice_fusion, bf16[256,128]{1,0:T(8,128)(2,1)} %param.6), kind=kOutput, calls=%fused_computation.29 | convolution fusion | flops 100663296 | bytes 1638400 | tf_op jit(solution)/shard_map/dot_general | solution.py:29
  48.4 0.0 collective-permute-done.5
  48.4 0.2 dynamic-slice_add_fusion
  48.6 0.0 copy-done.1
  48.6 0.1 fusion.1
  48.7 0.1 constant_dynamic-slice_fusion.1
  48.9 5.2 %all_gather.22 = bf16[2,2,768,128]{3,2,1,0:T(8,128)(2,1)S(1)} all-gather(bf16[1,2,768,128]{3,2,1,0:T(8,128)(2,1)S(1)} %pad_maximum_fusion.3), channel_id=1, replica_groups=mesh['y'=8,'x'=4,'core'=2,'zl'=4,'zh'=2] {'core'}, dimensions={0}, use_global_device_ids=true | all-gather | bytes 1179648 | tf_op jit(solution)/shard_map/all_gather | solution.py:180
  54.0 0.1 pad_maximum_fusion.1
  54.1 0.0 slice-start
  54.2 0.0 copy-start.5
  54.2 0.1 fusion
  54.3 0.5 slice-done
  54.8 0.9 pad_maximum_fusion.2
  55.7 1.9 %all-to-all-done = bf16[32,32,128]{2,1,0:T(8,128)(2,1)S(1)} async-done(((bf16[32,32,128]{2,1,0:T(8,128)(2,1)}), bf16[32,32,128]{2,1,0:T(8,128)(2,1)S(1)}, u32[]{:S(2)}, u32[]{:S(2)}) %all-to-all-start) | async-done | bytes 262176 | tf_op jit(solution)/shard_map/all_to_all | solution.py:164
  57.6 0.0 copy-start.4
  57.6 7.6 %all-to-all-start.1 = ((bf16[32,64,128]{2,1,0:T(8,128)(2,1)}), bf16[32,64,128]{2,1,0:T(8,128)(2,1)S(1)}, u32[]{:S(2)}, u32[]{:S(2)}) async-start(bf16[32,64,128]{2,1,0:T(8,128)(2,1)} %pad_maximum_fusion.2), calls=%async_computation.1 | async-start | bytes 1048576 | tf_op jit(solution)/shard_map/all_to_all | solution.py:186
  65.2 0.0 copy-done.5
  65.2 12.3 %all-gather = bf16[1024,128]{1,0:T(8,128)(2,1)S(1)} all-gather(bf16[256,128]{1,0:T(8,128)(2,1)S(1)} %copy-done.5), channel_id=2, replica_groups=mesh['y'=8,'x'=4,'core'=2,'zl'=4,'zh'=2] {'zl'}, dimensions={0}, use_global_device_ids=true | all-gather | bytes 327680 | tf_op jit(solution)/shard_map/all_gather | solution.py:187
  77.5 4.0 %all-to-all-done.1 = bf16[32,64,128]{2,1,0:T(8,128)(2,1)S(1)} async-done(((bf16[32,64,128]{2,1,0:T(8,128)(2,1)}), bf16[32,64,128]{2,1,0:T(8,128)(2,1)S(1)}, u32[]{:S(2)}, u32[]{:S(2)}) %all-to-all-start.1) | async-done | bytes 524320 | tf_op jit(solution)/shard_map/all_to_all | solution.py:186
  81.5 0.1 convert_reduce_fusion
  81.6 0.8 broadcast_in_dim.8
  82.4 0.0 copy-done.4
  82.4 5.2 %all-to-all-start.2 = ((bf16[32,48,128]{2,1,0:T(8,128)(2,1)}), bf16[32,48,128]{2,1,0:T(8,128)(2,1)S(1)}, u32[]{:S(2)}, u32[]{:S(2)}) async-start(bf16[32,48,128]{2,1,0:T(8,128)(2,1)} %broadcast_in_dim.8), calls=%async_computation.2 | async-start | bytes 786432 | tf_op jit(solution)/shard_map/all_to_all | solution.py:143
  87.6 0.1 pad_add_fusion.place_ref
  87.7 3.3 %collective-permute-start.6 = (bf16[4,256,128]{2,1,0:T(8,128)(2,1)S(1)}, bf16[4,256,128]{2,1,0:T(8,128)(2,1)S(1)}, u32[]{:S(2)}, u32[]{:S(2)}) collective-permute-start(bf16[4,256,128]{2,1,0:T(8,128)(2,1)S(1)} %bitcast.42), channel_id=1, source_target_pairs={{0,1},{1,0},{2,3},{3,2},{4,5},{5,4},{6,7},{7,6},{8,9},{9,8},{10,11... | collective-permute-start | bytes 786440 | tf_op jit(solution)/shard_map/ppermute | solution.py:134
  91.0 1.0 pad_maximum_fusion.4
  92.0 1.2 %convert_add_fusion = f32[4,1,384,128]{3,2,0,1:T(8,128)S(1)} fusion(bf16[4,1,384,128]{3,2,0,1:T(8,128)(2,1)S(1)} %bitcast.50, f32[4,2,384,128]{3,2,0,1:T(8,128)} %copy-done.1, s32[]{:T(128)S(6)} %select_n.59), kind=kLoop, calls=%fused_computation.3 | loop fusion | flops 393216 | bytes 1966084 | tf_op jit(solution)/shard_map/add | solution.py:171
  93.2 0.0 copy-start
  93.2 6.1 %all-gather.2 = bf16[64,48,128]{2,1,0:T(8,128)(2,1)S(1)} all-gather(bf16[32,48,128]{2,1,0:T(8,128)(2,1)S(1)} %pad_maximum_fusion.4), channel_id=4, replica_groups=mesh['y'=8,'x'=4,'core'=2,'zl'=4,'zh'=2] {'core'}, dimensions={0}, use_global_device_ids=true | all-gather | bytes 1179648 | tf_op jit(solution)/shard_map/all_gather | solution.py:196
  99.3 0.0 all-to-all-done.2
  99.3 7.0 %all-gather.1 = bf16[64,48,128]{2,1,0:T(8,128)(2,1)S(1)} all-gather(bf16[32,48,128]{2,1,0:T(8,128)(2,1)S(1)} %all-to-all-done.2), channel_id=3, replica_groups=mesh['y'=8,'x'=4,'core'=2,'zl'=4,'zh'=2] {'core'}, dimensions={0}, use_global_device_ids=true | all-gather | bytes 1179648 | tf_op jit(solution)/shard_map/all_gather | solution.py:197
  106.3 0.0 collective-permute-done.6.far_ref
  106.3 0.0 copy-done
  106.3 6.8 %basis_feedback_input_grad.1 = (f32[3072,128]{1,0:T(8,128)}, f32[32,128]{1,0:T(8,128)}, bf16[256,384]{1,0:T(8,128)(2,1)}) custom-call(s32[2]{0:T(128)S(1)} %pad_add_fusion.place_ref, bf16[3072,128]{1,0:T(8,128)(2,1)S(1)} %bitcast.41, f32[1536,128]{1,0:T(8,128)S(1)} %bitcast.38, f32[1536,128]{1,0:T(8,128)S(1)} %bitcast.39, f32[32,128]{1,0:T(8,128)S(1)} %bitcast.44, ...), custom_call_target="tpu_custom_call" | custom-call | flops 402653184 | bytes 5000000 | tf_op jit(solution)/shard_map/basis_feedback_input_grad/pallas_call | solution.py:109
  (10 shorter events, 0.2 us)
Async XLA Ops:
  0.6 27.7 %collective-permute-start.1 = (bf16[256,384]{1,0:T(8,128)(2,1)}, bf16[256,384]{1,0:T(8,128)(2,1)S(1)}, u32[]{:S(2)}, u32[]{:S(2)}) collective-permute-start(bf16[256,384]{1,0:T(8,128)(2,1)} %param.5), channel_id=1, source_target_pairs={{0,4},{2,6},{4,0},{6,2},{1,5},{3,7},{5,1},{7,3},{8,12},{10,14},{12... | collective-permute-start | bytes 589832 | tf_op jit(solution)/shard_map/ppermute | solution.py:157
  12.1 16.2 %collective-permute-start = (bf16[256,384]{1,0:T(8,128)(2,1)}, bf16[256,384]{1,0:T(8,128)(2,1)S(1)}, u32[]{:S(2)}, u32[]{:S(2)}) collective-permute-start(bf16[256,384]{1,0:T(8,128)(2,1)} %param.5), channel_id=1, source_target_pairs={{0,2},{2,4},{4,6},{6,0},{1,3},{3,5},{5,7},{7,1},{8,10},{10,12},{12... | collective-permute-start | bytes 589832 | tf_op jit(solution)/shard_map/ppermute | solution.py:157
  16.1 15.1 %collective-permute-start.2 = (bf16[256,384]{1,0:T(8,128)(2,1)}, bf16[256,384]{1,0:T(8,128)(2,1)S(1)}, u32[]{:S(2)}, u32[]{:S(2)}) collective-permute-start(bf16[256,384]{1,0:T(8,128)(2,1)} %param.5), channel_id=1, source_target_pairs={{0,6},{2,0},{4,2},{6,4},{1,7},{3,1},{5,3},{7,5},{8,14},{10,8},{12,... | collective-permute-start | bytes 589832 | tf_op jit(solution)/shard_map/ppermute | solution.py:157
  19.5 8.8 %collective-permute-start.3 = (bf16[48,128]{1,0:T(8,128)(2,1)}, bf16[48,128]{1,0:T(8,128)(2,1)S(1)}, u32[]{:S(2)}, u32[]{:S(2)}) collective-permute-start(bf16[48,128]{1,0:T(8,128)(2,1)} %param.7), channel_id=1, source_target_pairs={{0,0},{1,64},{2,128},{3,192},{4,256},{5,320},{6,384},{7,448},{64,1... | collective-permute-start | bytes 36872 | tf_op jit(solution)/shard_map/ppermute | solution.py:154
  20.9 12.0 %collective-permute-start.4 = (bf16[256,128]{1,0:T(8,128)(2,1)}, bf16[256,128]{1,0:T(8,128)(2,1)S(1)}, u32[]{:S(2)}, u32[]{:S(2)}) collective-permute-start(bf16[256,128]{1,0:T(8,128)(2,1)} %param.6), channel_id=1, source_target_pairs={{0,1},{1,0},{2,3},{3,2},{4,5},{5,4},{6,7},{7,6},{8,9},{9,8},{10,11... | collective-permute-start | bytes 196616 | tf_op jit(solution)/shard_map/ppermute | solution.py:134
  25.9 6.1 %copy-start.6 = (bf16[256,384]{1,0:T(8,128)(2,1)S(1)}, bf16[256,384]{1,0:T(8,128)(2,1)}, u32[]{:S(2)}) copy-start(bf16[256,384]{1,0:T(8,128)(2,1)} %param.5) | copy-start | bytes 589828
  28.3 8.8 %copy-start.2 = (f32[1,2,384,128]{3,2,0,1:T(8,128)S(1)}, f32[1,2,384,128]{3,2,0,1:T(8,128)}, u32[]{:S(2)}) copy-start(f32[1,2,384,128]{3,2,0,1:T(8,128)} %get-tuple-element.47) | copy-start | bytes 1179652
  28.3 8.8 %copy-start.3 = (f32[1,2,384,128]{3,2,0,1:T(8,128)S(1)}, f32[1,2,384,128]{3,2,0,1:T(8,128)}, u32[]{:S(2)}) copy-start(f32[1,2,384,128]{3,2,0,1:T(8,128)} %get-tuple-element.48) | copy-start | bytes 1179652
  28.3 9.0 %copy-start.7 = (bf16[48,128]{1,0:T(8,128)(2,1)}, bf16[48,128]{1,0:T(8,128)(2,1)S(1)}, u32[]{:S(2)}) copy-start(bf16[48,128]{1,0:T(8,128)(2,1)S(1)} %collective-permute-done.3) | copy-start | bytes 36868
  34.0 14.4 %collective-permute-start.5 = (bf16[1536,128]{1,0:T(8,128)(2,1)}, bf16[1536,128]{1,0:T(8,128)(2,1)S(1)}, u32[]{:S(2)}, u32[]{:S(2)}) collective-permute-start(bf16[1536,128]{1,0:T(8,128)(2,1)} %convolution_convert_fusion), channel_id=1, source_target_pairs={{0,1},{1,0},{2,3},{3,2},{4,5},{5,4},{6,7},{7,6},{8,9},{9,8},{10,11... | collective-permute-start | bytes 1179656 | tf_op jit(solution)/shard_map/ppermute | solution.py:134
  37.2 11.4 %copy-start.1 = (f32[4,2,384,128]{3,2,0,1:T(8,128)}, f32[4,2,384,128]{3,2,0,1:T(8,128)S(1)}, u32[]{:S(2)}) copy-start(f32[4,2,384,128]{3,2,0,1:T(8,128)S(1)} %pad_maximum_fusion) | copy-start | bytes 4718596
  37.2 20.3 %all-to-all-start = ((bf16[32,32,128]{2,1,0:T(8,128)(2,1)}), bf16[32,32,128]{2,1,0:T(8,128)(2,1)S(1)}, u32[]{:S(2)}, u32[]{:S(2)}) async-start(bf16[32,32,128]{2,1,0:T(8,128)(2,1)} %broadcast_in_dim.6), calls=%async_computation | async-start | bytes 524288 | tf_op jit(solution)/shard_map/all_to_all | solution.py:164
  54.1 0.7 slice-start
  54.2 11.0 %copy-start.5 = (bf16[256,128]{1,0:T(8,128)(2,1)S(1)}, bf16[256,128]{1,0:T(8,128)(2,1)}, u32[]{:S(2)}) copy-start(bf16[256,128]{1,0:T(8,128)(2,1)} %param.6) | copy-start | bytes 196612
  57.6 24.8 %copy-start.4 = (bf16[32,32,128]{2,1,0:T(8,128)(2,1)}, bf16[32,32,128]{2,1,0:T(8,128)(2,1)S(1)}, u32[]{:S(2)}) copy-start(bf16[32,32,128]{2,1,0:T(8,128)(2,1)S(1)} %all-to-all-done) | copy-start | bytes 786436
  57.6 24.0 %all-to-all-start.1 = ((bf16[32,64,128]{2,1,0:T(8,128)(2,1)}), bf16[32,64,128]{2,1,0:T(8,128)(2,1)S(1)}, u32[]{:S(2)}, u32[]{:S(2)}) async-start(bf16[32,64,128]{2,1,0:T(8,128)(2,1)} %pad_maximum_fusion.2), calls=%async_computation.1 | async-start | bytes 1048576 | tf_op jit(solution)/shard_map/all_to_all | solution.py:186
  82.4 16.9 %all-to-all-start.2 = ((bf16[32,48,128]{2,1,0:T(8,128)(2,1)}), bf16[32,48,128]{2,1,0:T(8,128)(2,1)S(1)}, u32[]{:S(2)}, u32[]{:S(2)}) async-start(bf16[32,48,128]{2,1,0:T(8,128)(2,1)} %broadcast_in_dim.8), calls=%async_computation.2 | async-start | bytes 786432 | tf_op jit(solution)/shard_map/all_to_all | solution.py:143
  87.7 18.6 %collective-permute-start.6 = (bf16[4,256,128]{2,1,0:T(8,128)(2,1)S(1)}, bf16[4,256,128]{2,1,0:T(8,128)(2,1)S(1)}, u32[]{:S(2)}, u32[]{:S(2)}) collective-permute-start(bf16[4,256,128]{2,1,0:T(8,128)(2,1)S(1)} %bitcast.42), channel_id=1, source_target_pairs={{0,1},{1,0},{2,3},{3,2},{4,5},{5,4},{6,7},{7,6},{8,9},{9,8},{10,11... | collective-permute-start | bytes 786440 | tf_op jit(solution)/shard_map/ppermute | solution.py:134
  93.2 13.2 %copy-start = (f32[128,32]{0,1:T(8,128)S(1)}, f32[128,32]{0,1:T(8,128)}, u32[]{:S(2)}) copy-start(f32[128,32]{0,1:T(8,128)} %param.9) | copy-start | bytes 49156

commit v7 on v6

--- a/solution.py
+++ b/solution.py
@@ -22,7 +22,7 @@
 TOK = 256
 COLS = 128
 RANK = 32
-EARLY = 32
+EARLY = 24
 
 
 def dot(a, b, dims, precision=None):

time: 114 us -> 114 us (level)
  waiting for transfers between devices: 9.58 us -> 14.4 us
  blocking collectives: 30.6 us -> 27.6 us
    all_to_all x1, waiting for transfers between devices: 0.01 us -> 3.54 us  [to_all_chips(): return lax.all_to_all(spread, CHIPS, 0, 0)]
    all_gather x1, blocking collectives: 7.03 us -> 5.31 us  [on_device(): lax.all_gather(to_all_chips(piece), 'core', axis=0).reshape(D_IN, COLS)]
    all_gather x1, blocking collectives: 6.1 us -> 4.75 us  [on_device(): weights = lax.all_gather(chip_weights, 'core', axis=0)]
    all_to_all x1, waiting for transfers between devices: 4.03 us -> 5.22 us  [on_device(): arrived = lax.all_to_all(load, CHIPS, 0, 0)]
    unnamed x20 -> x16, local copies, waits for them, and re-layouts: 2.51 us -> 2.51 us
  transfers between devices with their start and end apart: 10 -> 10, of which waited for: 4 -> 5; matrix products, arithmetic and copies ran while one was open for 7% -> 7% of each run, Pallas kernels for 0% -> 0%
where the time goes in v7:
time: 114 us; the launch traced here: 113 us
  starting transfers between devices  54.2 us (48%)
  blocking collectives  27.6 us (24%)
  waiting for transfers between devices  14.4 us (13%)
  Pallas kernels  6.75 us (6%)
  local copies, waits for them, and re-layouts  4.3 us (4%)
  other arithmetic  2.74 us (2%)
  matrix products  2.42 us (2%)
    ppermute x3, starting transfers between devices, on_device(): lax.ppermute(features, 'zl', [(i, (i + k) % N_ZL) for i in range(N_ZL)])  18.9 us
    all_gather x1, blocking collectives, on_device(): near = lax.all_gather(late, 'zl', axis=0)  12.4 us
    ppermute x3, starting transfers between devices, swap_halves(): return lax.ppermute(block, 'zh', [(0, 1), (1, 0)])  11.2 us
    all_to_all x1, starting transfers between devices, on_device(): early_weights = lax.all_to_all(spread, CHIPS, 0, 0)  9.85 us
    all_to_all x1, starting transfers between devices, on_device(): arrived = lax.all_to_all(load, CHIPS, 0, 0)  7.6 us
    pallas_call x1, Pallas kernels, tail_call(): pl.pallas_call(tail_kernel, in_specs=[pl.BlockSpec(memory_space=pltpu.SME...  6.75 us
    all_to_all x1, starting transfers between devices, to_all_chips(): return lax.all_to_all(spread, CHIPS, 0, 0)  5.32 us
    all_gather x1, blocking collectives, on_device(): lax.all_gather(to_all_chips(piece), 'core', axis=0).reshape(D_IN, COLS)  5.31 us
  transfers between devices with their start and end apart: 10, of which 5 were waited for; matrix products, arithmetic and copies ran while one was open for 7% of the time, Pallas kernels for 0%

profile of v7, /device:TPU:1, one launch (start us, length us, event | category | flops | bytes accessed | tf_op | source)
XLA Modules:
  0.0 113.4 jit_solution(192936639071188816)
XLA Ops:
  0.6 11.5 %collective-permute-start.1 = (bf16[256,384]{1,0:T(8,128)(2,1)}, bf16[256,384]{1,0:T(8,128)(2,1)S(1)}, u32[]{:S(2)}, u32[]{:S(2)}) collective-permute-start(bf16[256,384]{1,0:T(8,128)(2,1)} %param.5), channel_id=1, source_target_pairs={{0,4},{2,6},{4,0},{6,2},{1,5},{3,7},{5,1},{7,3},{8,12},{10,14},{12... | collective-permute-start | bytes 589832 | tf_op jit(solution)/shard_map/ppermute | solution.py:157
  12.1 4.0 %collective-permute-start = (bf16[256,384]{1,0:T(8,128)(2,1)}, bf16[256,384]{1,0:T(8,128)(2,1)S(1)}, u32[]{:S(2)}, u32[]{:S(2)}) collective-permute-start(bf16[256,384]{1,0:T(8,128)(2,1)} %param.5), channel_id=1, source_target_pairs={{0,2},{2,4},{4,6},{6,0},{1,3},{3,5},{5,7},{7,1},{8,10},{10,12},{12... | collective-permute-start | bytes 589832 | tf_op jit(solution)/shard_map/ppermute | solution.py:157
  16.1 3.4 %collective-permute-start.2 = (bf16[256,384]{1,0:T(8,128)(2,1)}, bf16[256,384]{1,0:T(8,128)(2,1)S(1)}, u32[]{:S(2)}, u32[]{:S(2)}) collective-permute-start(bf16[256,384]{1,0:T(8,128)(2,1)} %param.5), channel_id=1, source_target_pairs={{0,6},{2,0},{4,2},{6,4},{1,7},{3,1},{5,3},{7,5},{8,14},{10,8},{12,... | collective-permute-start | bytes 589832 | tf_op jit(solution)/shard_map/ppermute | solution.py:157
  19.5 1.4 %collective-permute-start.3 = (bf16[48,128]{1,0:T(8,128)(2,1)}, bf16[48,128]{1,0:T(8,128)(2,1)S(1)}, u32[]{:S(2)}, u32[]{:S(2)}) collective-permute-start(bf16[48,128]{1,0:T(8,128)(2,1)} %param.7), channel_id=1, source_target_pairs={{0,0},{1,64},{2,128},{3,192},{4,256},{5,320},{6,384},{7,448},{64,1... | collective-permute-start | bytes 36872 | tf_op jit(solution)/shard_map/ppermute | solution.py:154
  20.9 4.9 %collective-permute-start.4 = (bf16[256,128]{1,0:T(8,128)(2,1)}, bf16[256,128]{1,0:T(8,128)(2,1)S(1)}, u32[]{:S(2)}, u32[]{:S(2)}) collective-permute-start(bf16[256,128]{1,0:T(8,128)(2,1)} %param.6), channel_id=1, source_target_pairs={{0,1},{1,0},{2,3},{3,2},{4,5},{5,4},{6,7},{7,6},{8,9},{9,8},{10,11... | collective-permute-start | bytes 196616 | tf_op jit(solution)/shard_map/ppermute | solution.py:134
  25.9 0.0 copy-start.5
  25.9 2.4 %dynamic-slice_bitcast_fusion.3 = (f32[1,2,384,128]{3,2,0,1:T(8,128)S(1)}, f32[1,2,384,128]{3,2,0,1:T(8,128)S(1)}, f32[1,2,384,128]{3,2,0,1:T(8,128)}, f32[1,2,384,128]{3,2,0,1:T(8,128)}) fusion(f32[4,2,384,128]{3,2,1,0:T(8,128)} %bitcast.51, s32[]{:T(128)S(6)} %select_n.50, s32[]{:T(128)S(6)} %select_n.54, s32[]{:T(128)S(6)} %select_n.52, s32[]{:T(128)S(6)} %select_n.56), kind=kLoop, calls=%fused_computation.17 | loop fusion | bytes 3145744
  28.3 0.0 copy-start.2
  28.3 0.0 copy-start.3
  28.3 0.0 collective-permute-done.3
  28.3 0.0 collective-permute-done.1
  28.3 0.0 collective-permute-done
  28.3 2.9 %collective-permute-done.2 = bf16[256,384]{1,0:T(8,128)(2,1)S(1)} collective-permute-done((bf16[256,384]{1,0:T(8,128)(2,1)}, bf16[256,384]{1,0:T(8,128)(2,1)S(1)}, u32[]{:S(2)}, u32[]{:S(2)}) %collective-permute-start.2) | collective-permute-done | bytes 196640 | tf_op jit(solution)/shard_map/ppermute | solution.py:157
  31.2 0.7 broadcast_in_dim.6
  31.9 0.0 copy-done.5
  32.1 0.8 collective-permute-done.4
  32.9 1.2 %convolution_convert_fusion = bf16[1536,128]{1,0:T(8,128)(2,1)} fusion(bf16[256,1536]{1,0:T(8,128)(2,1)S(1)} %constant_dynamic-update-slice_fusion, bf16[256,128]{1,0:T(8,128)(2,1)S(1)} %collective-permute-done.4), kind=kOutput, calls=%fused_computation | convolution fusion | flops 100859904 | bytes 1245184 | tf_op jit(solution)/shard_map/dot_general | solution.py:29
  34.0 3.1 %collective-permute-start.5 = (bf16[1536,128]{1,0:T(8,128)(2,1)}, bf16[1536,128]{1,0:T(8,128)(2,1)S(1)}, u32[]{:S(2)}, u32[]{:S(2)}) collective-permute-start(bf16[1536,128]{1,0:T(8,128)(2,1)} %convolution_convert_fusion), channel_id=1, source_target_pairs={{0,1},{1,0},{2,3},{3,2},{4,5},{5,4},{6,7},{7,6},{8,9},{9,8},{10,11... | collective-permute-start | bytes 1179656 | tf_op jit(solution)/shard_map/ppermute | solution.py:134
  37.1 0.0 copy-done.2
  37.1 0.0 copy-done.3
  37.1 0.1 pad_maximum_fusion
  37.2 0.0 copy-start.1
  37.3 9.9 %all-to-all-start = ((bf16[32,24,128]{2,1,0:T(8,128)(2,1)}), bf16[32,24,128]{2,1,0:T(8,128)(2,1)S(1)}, u32[]{:S(2)}, u32[]{:S(2)}) async-start(bf16[32,24,128]{2,1,0:T(8,128)(2,1)} %broadcast_in_dim.6), calls=%async_computation | async-start | bytes 393216 | tf_op jit(solution)/shard_map/all_to_all | solution.py:164
  47.1 1.2 %fusion.4 = f32[1536,128]{1,0:T(8,128)S(1)} fusion(bf16[256,1536]{1,0:T(8,128)(2,1)S(1)} %constant_dynamic-update-slice_fusion, bf16[256,128]{1,0:T(8,128)(2,1)} %param.6), kind=kOutput, calls=%fused_computation.30 | convolution fusion | flops 100663296 | bytes 1638400 | tf_op jit(solution)/shard_map/dot_general | solution.py:29
  48.4 0.0 collective-permute-done.5
  48.4 0.2 dynamic-slice_add_fusion
  48.6 0.0 copy-done.1
  48.6 0.1 fusion.1
  48.7 0.1 constant_dynamic-slice_fusion.1
  48.8 5.2 %all_gather.22 = bf16[2,2,768,128]{3,2,1,0:T(8,128)(2,1)S(1)} all-gather(bf16[1,2,768,128]{3,2,1,0:T(8,128)(2,1)S(1)} %pad_maximum_fusion.3), channel_id=1, replica_groups=mesh['y'=8,'x'=4,'core'=2,'zl'=4,'zh'=2] {'core'}, dimensions={0}, use_global_device_ids=true | all-gather | bytes 1179648 | tf_op jit(solution)/shard_map/all_gather | solution.py:180
  54.0 0.1 pad_maximum_fusion.1
  54.1 0.1 fusion
  54.2 0.0 copy-start.4
  54.2 0.9 pad_maximum_fusion.2
  55.1 1.9 %all-to-all-done = bf16[32,24,128]{2,1,0:T(8,128)(2,1)S(1)} async-done(((bf16[32,24,128]{2,1,0:T(8,128)(2,1)}), bf16[32,24,128]{2,1,0:T(8,128)(2,1)S(1)}, u32[]{:S(2)}, u32[]{:S(2)}) %all-to-all-start) | async-done | bytes 196640 | tf_op jit(solution)/shard_map/all_to_all | solution.py:164
  57.0 7.6 %all-to-all-start.1 = ((bf16[32,72,128]{2,1,0:T(8,128)(2,1)}), bf16[32,72,128]{2,1,0:T(8,128)(2,1)S(1)}, u32[]{:S(2)}, u32[]{:S(2)}) async-start(bf16[32,72,128]{2,1,0:T(8,128)(2,1)} %pad_maximum_fusion.2), calls=%async_computation.1 | async-start | bytes 1179648 | tf_op jit(solution)/shard_map/all_to_all | solution.py:186
  64.6 0.0 copy-done.4
  64.6 12.4 %all-gather = bf16[1024,128]{1,0:T(8,128)(2,1)S(1)} all-gather(bf16[256,128]{1,0:T(8,128)(2,1)S(1)} %copy-done.4), channel_id=2, replica_groups=mesh['y'=8,'x'=4,'core'=2,'zl'=4,'zh'=2] {'zl'}, dimensions={0}, use_global_device_ids=true | all-gather | bytes 327680 | tf_op jit(solution)/shard_map/all_gather | solution.py:187
  77.0 5.2 %all-to-all-done.1 = bf16[32,72,128]{2,1,0:T(8,128)(2,1)S(1)} async-done(((bf16[32,72,128]{2,1,0:T(8,128)(2,1)}), bf16[32,72,128]{2,1,0:T(8,128)(2,1)S(1)}, u32[]{:S(2)}, u32[]{:S(2)}) %all-to-all-start.1) | async-done | bytes 589856 | tf_op jit(solution)/shard_map/all_to_all | solution.py:186
  82.2 0.1 convert_reduce_fusion
  82.3 0.8 broadcast_in_dim.8
  83.1 5.3 %all-to-all-start.2 = ((bf16[32,48,128]{2,1,0:T(8,128)(2,1)}), bf16[32,48,128]{2,1,0:T(8,128)(2,1)S(1)}, u32[]{:S(2)}, u32[]{:S(2)}) async-start(bf16[32,48,128]{2,1,0:T(8,128)(2,1)} %broadcast_in_dim.8), calls=%async_computation.2 | async-start | bytes 786432 | tf_op jit(solution)/shard_map/all_to_all | solution.py:143
  88.4 0.1 pad_add_fusion.place_ref
  88.5 3.2 %collective-permute-start.6 = (bf16[4,256,128]{2,1,0:T(8,128)(2,1)S(1)}, bf16[4,256,128]{2,1,0:T(8,128)(2,1)S(1)}, u32[]{:S(2)}, u32[]{:S(2)}) collective-permute-start(bf16[4,256,128]{2,1,0:T(8,128)(2,1)S(1)} %bitcast.42), channel_id=1, source_target_pairs={{0,1},{1,0},{2,3},{3,2},{4,5},{5,4},{6,7},{7,6},{8,9},{9,8},{10,11... | collective-permute-start | bytes 786440 | tf_op jit(solution)/shard_map/ppermute | solution.py:134
  91.8 1.2 %convert_add_fusion = f32[4,1,384,128]{3,2,0,1:T(8,128)S(1)} fusion(bf16[4,1,384,128]{3,2,0,1:T(8,128)(2,1)S(1)} %bitcast.50, f32[4,2,384,128]{3,2,0,1:T(8,128)} %copy-done.1, s32[]{:T(128)S(6)} %select_n.59), kind=kLoop, calls=%fused_computation.3 | loop fusion | flops 393216 | bytes 1966084 | tf_op jit(solution)/shard_map/add | solution.py:171
  93.0 0.0 copy-start
  93.1 4.7 %all-gather.2 = bf16[64,48,128]{2,1,0:T(8,128)(2,1)S(1)} all-gather(bf16[32,48,128]{2,1,0:T(8,128)(2,1)S(1)} %pad_maximum_fusion.4), channel_id=4, replica_groups=mesh['y'=8,'x'=4,'core'=2,'zl'=4,'zh'=2] {'core'}, dimensions={0}, use_global_device_ids=true | all-gather | bytes 1179648 | tf_op jit(solution)/shard_map/all_gather | solution.py:196
  97.8 3.5 %all-to-all-done.2 = bf16[32,48,128]{2,1,0:T(8,128)(2,1)S(1)} async-done(((bf16[32,48,128]{2,1,0:T(8,128)(2,1)}), bf16[32,48,128]{2,1,0:T(8,128)(2,1)S(1)}, u32[]{:S(2)}, u32[]{:S(2)}) %all-to-all-start.2) | async-done | bytes 393248 | tf_op jit(solution)/shard_map/all_to_all | solution.py:143
  101.3 5.3 %all-gather.1 = bf16[64,48,128]{2,1,0:T(8,128)(2,1)S(1)} all-gather(bf16[32,48,128]{2,1,0:T(8,128)(2,1)S(1)} %all-to-all-done.2), channel_id=3, replica_groups=mesh['y'=8,'x'=4,'core'=2,'zl'=4,'zh'=2] {'core'}, dimensions={0}, use_global_device_ids=true | all-gather | bytes 1179648 | tf_op jit(solution)/shard_map/all_gather | solution.py:197
  106.7 0.0 collective-permute-done.6.far_ref
  106.7 0.0 copy-done
  106.7 6.8 %basis_feedback_input_grad.1 = (f32[3072,128]{1,0:T(8,128)}, f32[32,128]{1,0:T(8,128)}, bf16[256,384]{1,0:T(8,128)(2,1)}) custom-call(s32[2]{0:T(128)S(1)} %pad_add_fusion.place_ref, bf16[3072,128]{1,0:T(8,128)(2,1)S(1)} %bitcast.41, f32[1536,128]{1,0:T(8,128)S(1)} %bitcast.38, f32[1536,128]{1,0:T(8,128)S(1)} %bitcast.39, f32[32,128]{1,0:T(8,128)S(1)} %bitcast.44, ...), custom_call_target="tpu_custom_call" | custom-call | flops 402653184 | bytes 5000000 | tf_op jit(solution)/shard_map/basis_feedback_input_grad/pallas_call | solution.py:109
  (11 shorter events, 0.3 us)
Async XLA Ops:
  0.6 27.7 %collective-permute-start.1 = (bf16[256,384]{1,0:T(8,128)(2,1)}, bf16[256,384]{1,0:T(8,128)(2,1)S(1)}, u32[]{:S(2)}, u32[]{:S(2)}) collective-permute-start(bf16[256,384]{1,0:T(8,128)(2,1)} %param.5), channel_id=1, source_target_pairs={{0,4},{2,6},{4,0},{6,2},{1,5},{3,7},{5,1},{7,3},{8,12},{10,14},{12... | collective-permute-start | bytes 589832 | tf_op jit(solution)/shard_map/ppermute | solution.py:157
  12.1 16.2 %collective-permute-start = (bf16[256,384]{1,0:T(8,128)(2,1)}, bf16[256,384]{1,0:T(8,128)(2,1)S(1)}, u32[]{:S(2)}, u32[]{:S(2)}) collective-permute-start(bf16[256,384]{1,0:T(8,128)(2,1)} %param.5), channel_id=1, source_target_pairs={{0,2},{2,4},{4,6},{6,0},{1,3},{3,5},{5,7},{7,1},{8,10},{10,12},{12... | collective-permute-start | bytes 589832 | tf_op jit(solution)/shard_map/ppermute | solution.py:157
  16.1 15.1 %collective-permute-start.2 = (bf16[256,384]{1,0:T(8,128)(2,1)}, bf16[256,384]{1,0:T(8,128)(2,1)S(1)}, u32[]{:S(2)}, u32[]{:S(2)}) collective-permute-start(bf16[256,384]{1,0:T(8,128)(2,1)} %param.5), channel_id=1, source_target_pairs={{0,6},{2,0},{4,2},{6,4},{1,7},{3,1},{5,3},{7,5},{8,14},{10,8},{12,... | collective-permute-start | bytes 589832 | tf_op jit(solution)/shard_map/ppermute | solution.py:157
  19.5 8.8 %collective-permute-start.3 = (bf16[48,128]{1,0:T(8,128)(2,1)}, bf16[48,128]{1,0:T(8,128)(2,1)S(1)}, u32[]{:S(2)}, u32[]{:S(2)}) collective-permute-start(bf16[48,128]{1,0:T(8,128)(2,1)} %param.7), channel_id=1, source_target_pairs={{0,0},{1,64},{2,128},{3,192},{4,256},{5,320},{6,384},{7,448},{64,1... | collective-permute-start | bytes 36872 | tf_op jit(solution)/shard_map/ppermute | solution.py:154
  20.9 12.0 %collective-permute-start.4 = (bf16[256,128]{1,0:T(8,128)(2,1)}, bf16[256,128]{1,0:T(8,128)(2,1)S(1)}, u32[]{:S(2)}, u32[]{:S(2)}) collective-permute-start(bf16[256,128]{1,0:T(8,128)(2,1)} %param.6), channel_id=1, source_target_pairs={{0,1},{1,0},{2,3},{3,2},{4,5},{5,4},{6,7},{7,6},{8,9},{9,8},{10,11... | collective-permute-start | bytes 196616 | tf_op jit(solution)/shard_map/ppermute | solution.py:134
  25.9 6.0 %copy-start.5 = (bf16[256,384]{1,0:T(8,128)(2,1)S(1)}, bf16[256,384]{1,0:T(8,128)(2,1)}, u32[]{:S(2)}) copy-start(bf16[256,384]{1,0:T(8,128)(2,1)} %param.5) | copy-start | bytes 589828
  28.3 8.8 %copy-start.2 = (f32[1,2,384,128]{3,2,0,1:T(8,128)S(1)}, f32[1,2,384,128]{3,2,0,1:T(8,128)}, u32[]{:S(2)}) copy-start(f32[1,2,384,128]{3,2,0,1:T(8,128)} %get-tuple-element.47) | copy-start | bytes 1179652
  28.3 8.8 %copy-start.3 = (f32[1,2,384,128]{3,2,0,1:T(8,128)S(1)}, f32[1,2,384,128]{3,2,0,1:T(8,128)}, u32[]{:S(2)}) copy-start(f32[1,2,384,128]{3,2,0,1:T(8,128)} %get-tuple-element.48) | copy-start | bytes 1179652
  34.0 14.3 %collective-permute-start.5 = (bf16[1536,128]{1,0:T(8,128)(2,1)}, bf16[1536,128]{1,0:T(8,128)(2,1)S(1)}, u32[]{:S(2)}, u32[]{:S(2)}) collective-permute-start(bf16[1536,128]{1,0:T(8,128)(2,1)} %convolution_convert_fusion), channel_id=1, source_target_pairs={{0,1},{1,0},{2,3},{3,2},{4,5},{5,4},{6,7},{7,6},{8,9},{9,8},{10,11... | collective-permute-start | bytes 1179656 | tf_op jit(solution)/shard_map/ppermute | solution.py:134
  37.2 11.3 %copy-start.1 = (f32[4,2,384,128]{3,2,0,1:T(8,128)}, f32[4,2,384,128]{3,2,0,1:T(8,128)S(1)}, u32[]{:S(2)}) copy-start(f32[4,2,384,128]{3,2,0,1:T(8,128)S(1)} %pad_maximum_fusion) | copy-start | bytes 4718596
  37.3 19.7 %all-to-all-start = ((bf16[32,24,128]{2,1,0:T(8,128)(2,1)}), bf16[32,24,128]{2,1,0:T(8,128)(2,1)S(1)}, u32[]{:S(2)}, u32[]{:S(2)}) async-start(bf16[32,24,128]{2,1,0:T(8,128)(2,1)} %broadcast_in_dim.6), calls=%async_computation | async-start | bytes 393216 | tf_op jit(solution)/shard_map/all_to_all | solution.py:164
  54.2 10.4 %copy-start.4 = (bf16[256,128]{1,0:T(8,128)(2,1)S(1)}, bf16[256,128]{1,0:T(8,128)(2,1)}, u32[]{:S(2)}) copy-start(bf16[256,128]{1,0:T(8,128)(2,1)} %param.6) | copy-start | bytes 196612
  57.0 25.2 %all-to-all-start.1 = ((bf16[32,72,128]{2,1,0:T(8,128)(2,1)}), bf16[32,72,128]{2,1,0:T(8,128)(2,1)S(1)}, u32[]{:S(2)}, u32[]{:S(2)}) async-start(bf16[32,72,128]{2,1,0:T(8,128)(2,1)} %pad_maximum_fusion.2), calls=%async_computation.1 | async-start | bytes 1179648 | tf_op jit(solution)/shard_map/all_to_all | solution.py:186
  83.1 18.2 %all-to-all-start.2 = ((bf16[32,48,128]{2,1,0:T(8,128)(2,1)}), bf16[32,48,128]{2,1,0:T(8,128)(2,1)S(1)}, u32[]{:S(2)}, u32[]{:S(2)}) async-start(bf16[32,48,128]{2,1,0:T(8,128)(2,1)} %broadcast_in_dim.8), calls=%async_computation.2 | async-start | bytes 786432 | tf_op jit(solution)/shard_map/all_to_all | solution.py:143
  88.5 18.1 %collective-permute-start.6 = (bf16[4,256,128]{2,1,0:T(8,128)(2,1)S(1)}, bf16[4,256,128]{2,1,0:T(8,128)(2,1)S(1)}, u32[]{:S(2)}, u32[]{:S(2)}) collective-permute-start(bf16[4,256,128]{2,1,0:T(8,128)(2,1)S(1)} %bitcast.42), channel_id=1, source_target_pairs={{0,1},{1,0},{2,3},{3,2},{4,5},{5,4},{6,7},{7,6},{8,9},{9,8},{10,11... | collective-permute-start | bytes 786440 | tf_op jit(solution)/shard_map/ppermute | solution.py:134
  93.0 13.6 %copy-start = (f32[128,32]{0,1:T(8,128)S(1)}, f32[128,32]{0,1:T(8,128)}, u32[]{:S(2)}) copy-start(f32[128,32]{0,1:T(8,128)} %param.9) | copy-start | bytes 49156
